TPU v7x, 512 devices: a whole 4x8x8 slice. The times are simulated.
512 devices in a mesh: seq: 64 (over z, y), head: 8 (over x, core).
Axes of the slice: x: 4, y: 8, z: 8, core: 2. Of those that a mesh axis runs over, the one named last changes fastest.
Arguments:
- raw_keys: bfloat16 [2, 65536, 8, 128], P(None, 'seq', 'head'), may hold values from -6 to 6
- raw_values: bfloat16 [2, 65536, 8, 128], P(None, 'seq', 'head'), may hold values from -6 to 6
- phase: int32 [2], replicated, may hold values from 0 to 255, as said below
- ratio: int32 [2, 64], replicated, may hold values from 8 to 32, as said below
- resident_len: int32 [2, 64], replicated, may hold values from 1 to 256, as said below
- beacon_queries: bfloat16 [2, 8192, 8, 8, 128], P(None, 'seq', 'head'), may hold values from -150 to 150
- beacon_wk: bfloat16 [8192, 1024], P('seq', 'head'), may hold values from -0.125 to 0.125
- beacon_wv: bfloat16 [8192, 1024], P('seq', 'head'), may hold values from -0.125 to 0.125
- resident_keys: bfloat16 [2, 16384, 8, 128], P(None, 'seq', 'head'), may hold values from -6 to 6
- resident_values: bfloat16 [2, 16384, 8, 128], P(None, 'seq', 'head'), may hold values from -6 to 6
- decode_queries: bfloat16 [4, 2, 8, 8, 128], P(None, None, 'head'), may hold values from -150 to 150
- out_weight: bfloat16 [8192, 8192], P('head', 'seq'), may hold values from -0.0625 to 0.0625
Outputs:
- beacon_keys: bfloat16 [2, 8192, 8, 128], P(None, 'seq', 'head')
- beacon_values: bfloat16 [2, 8192, 8, 128], P(None, 'seq', 'head')
- projected: bfloat16 [4, 2, 8192], P(None, None, 'seq')
Inputs may be any that keep to these rules, and one draw needn't show every extreme that they name: `phase`: some request has 255. `ratio`: each value is 1024 // 128 times 1, 2 or 4; both ends occur. `resident_len`: some pair has 256.
All inputs are finite; a program needn't handle non-finite values.
Results may differ from a plain program's by a relative error of at most 0.025.
Values may be sent and summed in bfloat16 or wider, within the bound.
No kernel may reach another device: no remote copies, remote signals or barrier semaphores. Data moves between devices by JAX's collectives and lax.ppermute only.
A program may use at most 64 MiB of HBM per device.

v0:
```python
import math

import jax
import jax.numpy as jnp
from jax import lax
from jax.sharding import PartitionSpec as P

G = 8
INTERVAL = 1024
NB = 128
OFF = 256
STEPS = 4


masked_score = -1e30


def shifted(value, axis, steps):
    count = lax.axis_size(axis)
    first, last = (max(0, -steps), min(count, count - steps))
    return lax.ppermute(value, axis, [(source, source + steps) for source in range(first, last)])


def pool_part(queries, key_rows, value_rows, positions, present, reaches):
    inv_root = 1.0 / math.sqrt(queries.shape[-1])

    def per_request(members):
        query_block, key_block, value_block, position_row, present_row, reach_row = members
        scores = (
            jnp.einsum("jkgd,ikd->jkgi", query_block, key_block, preferred_element_type=jnp.float32)
            * inv_root
        )
        allowed = (
            present_row[None, :]
            & (position_row[None, :] >= 0)
            & (position_row[None, :] < INTERVAL)
            & (position_row[None, :] < reach_row[:, None])
        )
        cache_mask = allowed[:, None, None, :]
        row_peak = jnp.max(jnp.where(cache_mask, scores, masked_score), axis=-1)
        weights = jnp.where(cache_mask, jnp.exp(scores - row_peak[..., None]), 0.0)
        weight_sum = jnp.sum(weights, axis=-1)
        weighted = jnp.einsum(
            "jkgi,ikd->jkgd",
            weights.astype(jnp.bfloat16),
            value_block,
            preferred_element_type=jnp.float32,
        )
        return (row_peak, weight_sum, weighted)

    return lax.map(per_request, (queries, key_rows, value_rows, positions, present, reaches))


def body(
    raw_keys,
    raw_values,
    phase,
    ratio,
    resident_len,
    beacon_queries,
    beacon_wk,
    beacon_wv,
    resident_keys,
    resident_values,
    decode_queries,
    out_weight,
):
    requests = raw_keys.shape[0]
    kv_local = raw_keys.shape[2]
    head_dim = raw_keys.shape[3]
    shard_index = lax.axis_index("seq")
    shard_count = lax.axis_size("seq")
    is_first = shard_index == 0
    is_last = shard_index == shard_count - 1
    own_ratio = lax.dynamic_index_in_dim(ratio, shard_index, 1, keepdims=False)
    slot_ids = jnp.arange(NB, dtype=jnp.int32)
    lead_in = jnp.where(is_first, phase, 0)
    reaches = (slot_ids[None, :] + 1) * own_ratio[:, None] + lead_in[:, None]
    tail_keys = raw_keys[:, INTERVAL - OFF :]
    tail_values = raw_values[:, INTERVAL - OFF :]
    own_positions = jnp.arange(INTERVAL, dtype=jnp.int32)[None, :] + phase[:, None]
    rim_ids = jnp.arange(OFF, dtype=jnp.int32)
    rim_positions = rim_ids[None, :] - OFF + phase[:, None]
    near_keys, near_values = shifted((tail_keys, tail_values), "seq", 1)
    key_rows = jnp.concatenate([near_keys, raw_keys], axis=1)
    value_rows = jnp.concatenate([near_values, raw_values], axis=1)
    positions = jnp.concatenate([rim_positions, own_positions], axis=1)
    present = jnp.logical_not(is_first) | (positions >= phase[:, None])
    pooled_parts = pool_part(beacon_queries, key_rows, value_rows, positions, present, reaches)
    pooled = (pooled_parts[2] / pooled_parts[1][..., None]).astype(jnp.bfloat16)
    pooled_flat = pooled.reshape(requests * NB, kv_local * G * head_dim)
    pooled_whole = lax.all_gather(pooled_flat, "head", axis=1, tiled=True)
    key_sum = jnp.dot(
        pooled_whole,
        lax.all_gather(beacon_wk, "seq", axis=0, tiled=True),
        preferred_element_type=jnp.float32,
    )
    value_sum = jnp.dot(
        pooled_whole,
        lax.all_gather(beacon_wv, "seq", axis=0, tiled=True),
        preferred_element_type=jnp.float32,
    )
    made_keys = key_sum
    made_values = value_sum
    made_keys = made_keys.reshape(requests, NB, kv_local, head_dim)
    made_values = made_values.reshape(requests, NB, kv_local, head_dim)
    slot_live = slot_ids[None, :] < (INTERVAL // own_ratio)[:, None]
    beacon_keys = jnp.where(slot_live[:, :, None, None], made_keys, 0.0).astype(jnp.bfloat16)
    beacon_values = jnp.where(slot_live[:, :, None, None], made_values, 0.0).astype(jnp.bfloat16)
    cache_keys = jnp.concatenate([resident_keys, beacon_keys, tail_keys], axis=1)
    cache_values = jnp.concatenate([resident_values, beacon_values, tail_values], axis=1)
    own_len = lax.dynamic_index_in_dim(resident_len, shard_index, 1, keepdims=False)
    resident_ok = jnp.arange(resident_keys.shape[1], dtype=jnp.int32)[None, :] < own_len[:, None]
    leftover_ok = (rim_ids[None, :] >= OFF - phase[:, None]) & is_last
    usable = jnp.concatenate([resident_ok, slot_live, leftover_ok], axis=1)
    inv_root = 1.0 / math.sqrt(head_dim)
    scores = (
        jnp.einsum(
            "srkgd,rikd->rksgi", decode_queries, cache_keys, preferred_element_type=jnp.float32
        )
        * inv_root
    )
    cache_mask = usable[:, None, None, None, :]
    row_peak = jnp.max(jnp.where(cache_mask, scores, masked_score), axis=-1)
    weights = jnp.where(cache_mask, jnp.exp(scores - row_peak[..., None]), 0.0)
    weight_sum = jnp.sum(weights, axis=-1)
    weighted = jnp.einsum(
        "rksgi,rikd->rksgd",
        weights.astype(jnp.bfloat16),
        cache_values,
        preferred_element_type=jnp.float32,
    )
    global_peak = lax.pmax(row_peak, "seq")
    rescale = jnp.exp(row_peak - global_peak)
    total_sum, total_weighted = lax.psum(
        (weight_sum * rescale, weighted * rescale[..., None]), "seq"
    )
    attended = (total_weighted / total_sum[..., None]).astype(jnp.bfloat16)
    attended = jnp.transpose(attended, (2, 0, 1, 3, 4)).reshape(
        STEPS * requests, kv_local * G * head_dim
    )
    partial_value = jnp.dot(attended, out_weight, preferred_element_type=jnp.float32)
    summed = lax.psum(partial_value, "head")
    projected = summed.astype(jnp.bfloat16).reshape(STEPS, requests, out_weight.shape[1])
    return (beacon_keys, beacon_values, projected)


def solution(mesh):
    return jax.shard_map(
        body,
        mesh=mesh,
        in_specs=(
            P(None, "seq", "head", None),
            P(None, "seq", "head", None),
            P(),
            P(),
            P(),
            P(None, "seq", "head", None, None),
            P("seq", "head"),
            P("seq", "head"),
            P(None, "seq", "head", None),
            P(None, "seq", "head", None),
            P(None, None, "head", None, None),
            P("head", "seq"),
        ),
        out_specs=(
            P(None, "seq", "head", None),
            P(None, "seq", "head", None),
            P(None, None, "seq"),
        ),
        check_vma=False,
    )
```

profile of v0, /device:TPU:1, one launch (start us, length us, event | category | flops | bytes accessed | tf_op | source)
XLA Modules:
  0.0 666.6 jit_solution(5328392180371530264)
XLA Ops:
  7.2 1.0 slice.9
  8.2 4.7 collective-permute-start.1
  12.9 0.9 slice.8
  13.8 2.6 collective-permute-start
  16.5 0.7 broadcast_subtract_fusion
  17.2 0.7 iota_add_fusion
  17.9 1.2 copy.32
  19.2 0.7 broadcast_add_fusion
  19.9 0.7 compare_or_fusion
  20.6 1.0 fusion.44
  21.8 1.1 pad_maximum_fusion
  22.9 1.0 copy.31
  23.9 0.9 pad_maximum_fusion.1
  24.8 8.6 %while.12 = (s32[]{:T(128)}, f32[2,128,1,8]{1,3,2,0:T(8,128)S(1)}, f32[2,128,1,8,128]{1,4,3,2,0:T(8,128)S(1)}, pred[2,1280]{1,0:T(4,128)(4,1)S(1)}, s32[2,1280]{...) while((s32[]{:T(128)}, f32[2,128,1,8]{1,3,2,0:T(8,128)S(1)}, ...), condition=%wide.region_3.4_spmd, body=%wide.region_0.3_spmd.sunk | while | flops 685837312 | bytes 21023128 | solution.py:51
  24.9 0.9 compare_and_fusion.3
  25.8 0.9 fusion.65
  26.8 1.2 fusion.67
  27.9 1.1 fusion.66
  29.2 0.9 compare_and_fusion.3
  30.2 0.9 fusion.65
  31.1 1.2 fusion.67
  32.3 1.1 fusion.66
  33.8 0.9 copy.60
  34.8 0.7 all-gather.8.cloned.1.call-update
  35.8 64.2 %all-gather.6.cloned.1.call-done = bf16[8192,128]{1,0:T(8,128)(2,1)} async-done(((bf16[128,128]{1,0:T(8,128)(2,1)}), bf16[8192,128]{1,0:T(8,128)(2,1)}) %all-gather.6.cloned.1.call-update) | async-done | bytes 2097168 | tf_op jit(solution)/shard_map/all_gather | solution.py:95
  99.9 40.7 %all-gather.4.cloned.1.call-done = bf16[256,8192]{1,0:T(8,128)(2,1)} async-done(((bf16[256,1024]{1,0:T(8,128)(2,1)}), bf16[256,8192]{1,0:T(8,128)(2,1)}) %all-gather.4.cloned.1.call-update) | async-done | bytes 4194320 | tf_op jit(solution)/shard_map/all_gather | solution.py:92
  140.6 4.1 fusion.48
  144.8 78.4 %all-gather.8.cloned.1.call-done = bf16[8192,128]{1,0:T(8,128)(2,1)} async-done(((bf16[128,128]{1,0:T(8,128)(2,1)}), bf16[8192,128]{1,0:T(8,128)(2,1)}) %all-gather.8.cloned.1.call-update) | async-done | bytes 2097168 | tf_op jit(solution)/shard_map/all_gather | solution.py:100
  223.1 4.1 fusion.49
  227.9 113.3 %pmax.7 = f32[2,1,4,8]{3,2,0,1:T(4,128)S(1)} all-reduce(f32[2,1,4,8]{3,2,0,1:T(4,128)S(1)} %bitcast.153), channel_id=1, replica_groups=mesh['seq'=64,'head'=8] {'seq'}, use_global_device_ids=true, to_apply=%region_5.6 | all-reduce | flops 64 | bytes 512 | tf_op jit(solution)/shard_map/pmax | solution.py:133
  341.5 219.7 %all-reduce = (f32[2,1,4,8,128]{4,3,2,0,1:T(8,128)S(1)}, f32[2,4,8]{2,1,0:T(4,128)S(1)}) all-reduce(f32[2,1,4,8,128]{4,3,2,0,1:T(8,128)S(1)} %fusion.25, f32[2,4,8]{2,1,0:T(4,128)S(1)} %get-tuple-element.101), channel_id=1, replica_groups=mesh['seq'=64,'head'=8] {'seq'}, use_global_device_ids=true, to_apply=%region_6.7 | all-reduce | flops 8256 | bytes 66048 | tf_op jit(solution)/shard_map/psum | solution.py:135
  561.5 98.6 %psum.23 = bf16[8,128]{1,0:T(8,128)(2,1)} all-reduce(f32[8,128]{1,0:T(8,128)S(1)} %fusion.37), channel_id=1, replica_groups=mesh['seq'=64,'head'=8] {'head'}, use_global_device_ids=true, to_apply=%region_9.10 | all-reduce | flops 1024 | bytes 6144 | tf_op jit(solution)/shard_map/psum | solution.py:143
  (55 shorter events, 2.3 us)
Async XLA Ops:
  7.2 554.2 %copy-start = (bf16[1024,128]{1,0:T(8,128)(2,1)S(1)}, bf16[1024,128]{1,0:T(8,128)(2,1)}, u32[]{:S(2)}) copy-start(bf16[1024,128]{1,0:T(8,128)(2,1)} %param.25) | copy-start | bytes 786436
  7.2 17.6 %copy-start.1 = (bf16[2,128,1,8,128]{4,3,2,1,0:T(8,128)(2,1)S(1)}, bf16[2,128,1,8,128]{4,3,2,1,0:T(8,128)(2,1)}, u32[]{:S(2)}) copy-start(bf16[2,128,1,8,128]{4,3,2,1,0:T(8,128)(2,1)} %param.19) | copy-start | bytes 1572868
  7.2 92.7 %all-gather.6.cloned.1.call-start = ((), (), s32[]{:S(2)}) async-start(), calls=%async_computation.1 | async-start | bytes 2129920 | tf_op jit(solution)/shard_map/all_gather | solution.py:95
  8.2 14.6 %collective-permute-start.1 = (bf16[2,256,1,128]{3,1,0,2:T(8,128)(2,1)S(1)}, bf16[2,256,1,128]{3,1,0,2:T(8,128)(2,1)}, u32[]{:S(2)}, u32[]{:S(2)}) collective-permute-start(bf16[2,256,1,128]{3,1,0,2:T(8,128)(2,1)S(1)} %slice.9), channel_id=1, source_target_pairs={{0,8},{8,16},{16,24},{24,32},{32,40},{40,48},{48,56},{56,64},{64,7... | collective-permute-start | bytes 393224 | tf_op jit(solution)/shard_map/ppermute | solution.py:21
  13.8 7.9 %collective-permute-start = (bf16[2,256,1,128]{3,1,0,2:T(8,128)(2,1)S(1)}, bf16[2,256,1,128]{3,1,0,2:T(8,128)(2,1)S(1)}, u32[]{:S(2)}, u32[]{:S(2)}) collective-permute-start(bf16[2,256,1,128]{3,1,0,2:T(8,128)(2,1)S(1)} %slice.8), channel_id=1, source_target_pairs={{0,8},{8,16},{16,24},{24,32},{32,40},{40,48},{48,56},{56,64},{64,7... | collective-permute-start | bytes 393224 | tf_op jit(solution)/shard_map/ppermute | solution.py:21
  16.4 124.2 %all-gather.4.cloned.1.call-start = ((), (), s32[]{:S(2)}) async-start(), calls=%async_computation | async-start | bytes 4718592 | tf_op jit(solution)/shard_map/all_gather | solution.py:92
  24.8 2.0 copy-start.2
  29.1 2.0 copy-start.2
  34.8 188.4 %all-gather.8.cloned.1.call-start = ((), (), s32[]{:S(2)}) async-start(), calls=%async_computation.2 | async-start | bytes 2129920 | tf_op jit(solution)/shard_map/all_gather | solution.py:100
  144.7 82.6 %copy-start.5 = (bf16[2,256,1,128]{3,1,2,0:T(8,128)(2,1)S(1)}, bf16[2,256,1,128]{3,1,2,0:T(8,128)(2,1)}, u32[]{:S(2)}) copy-start(bf16[2,256,1,128]{3,1,2,0:T(8,128)(2,1)} %param.22) | copy-start | bytes 393220
  144.8 82.6 %copy-start.7 = (bf16[4,2,1,8,128]{4,3,2,1,0:T(8,128)(2,1)S(1)}, bf16[4,2,1,8,128]{4,3,2,1,0:T(8,128)(2,1)}, u32[]{:S(2)}) copy-start(bf16[4,2,1,8,128]{4,3,2,1,0:T(8,128)(2,1)} %param.24) | copy-start | bytes 49156
  144.8 196.5 %copy-start.6 = (bf16[2,256,1,128]{3,1,2,0:T(8,128)(2,1)S(1)}, bf16[2,256,1,128]{3,1,2,0:T(8,128)(2,1)}, u32[]{:S(2)}) copy-start(bf16[2,256,1,128]{3,1,2,0:T(8,128)(2,1)} %param.23) | copy-start | bytes 393220
  227.4 432.7 %copy-start.3 = (bf16[2,128,1,128]{3,1,0,2:T(8,128)(2,1)}, bf16[2,128,1,128]{3,1,0,2:T(8,128)(2,1)S(1)}, u32[]{:S(2)}) copy-start(bf16[2,128,1,128]{3,1,0,2:T(8,128)(2,1)S(1)} %get-tuple-element.105) | copy-start | bytes 196612
  227.4 432.7 %copy-start.4 = (bf16[2,128,1,128]{3,1,0,2:T(8,128)(2,1)}, bf16[2,128,1,128]{3,1,0,2:T(8,128)(2,1)S(1)}, u32[]{:S(2)}) copy-start(bf16[2,128,1,128]{3,1,0,2:T(8,128)(2,1)S(1)} %get-tuple-element.106) | copy-start | bytes 196612
Sparse Core Ops, SparseCore 0:
  16.6 83.3 all-gather.5
  102.0 38.5 all-gather.3
  143.7 79.3 all-gather.7
where the time goes:
time: 667 us
  blocking collectives  432 us (65%)
  waiting for transfers between devices  184 us (28%)
  between operations  14 us (2%)
  matrix products  13.1 us (2%)
  other arithmetic  10.8 us (2%)
  starting transfers between devices  7.38 us (1%)
    psum x1, blocking collectives, body(): lax.psum((weight_sum * rescale, weighted * rescale[..., None]), 'seq')  220 us
    pmax x1, blocking collectives, body(): global_peak = lax.pmax(row_peak, 'seq')  113 us
    psum x1, blocking collectives, body(): summed = lax.psum(partial_value, 'head')  98.6 us
    all_gather x1, waiting for transfers between devices, body(): lax.all_gather(beacon_wv, 'seq', axis=0, tiled=True)  78.4 us
    all_gather x1, waiting for transfers between devices, body(): lax.all_gather(beacon_wk, 'seq', axis=0, tiled=True)  64.2 us
    all_gather x1, waiting for transfers between devices, body(): pooled_whole = lax.all_gather(pooled_flat, 'head', axis=1, tiled=True)  40.7 us
  transfers between devices with their start and end apart: 5, of which 3 were waited for; matrix products, arithmetic and copies ran while one was open for 3% of the time, Pallas kernels for 0%

commit v1 on v0

v1 whole, which is shorter than its diff:
```python
import math

import jax
import jax.numpy as jnp
from jax import lax
from jax.experimental import pallas as pl
from jax.experimental.pallas import tpu as pltpu
from jax.sharding import Mesh, PartitionSpec as P

G = 8
HD = 128
INTERVAL = 1024
NB = 128
OFF = 256
STEPS = 4
REQ = 2
RES = 256
ROWS = STEPS * REQ * G
SCALE = math.log2(math.e) / math.sqrt(HD)
MASKED = -1e30
SEQ = ("z", "y")
BF = jnp.bfloat16
F32 = jnp.float32


def dot_nt(a, b):
    return lax.dot_general(a, b, (((1,), (1,)), ((), ())), preferred_element_type=F32)


def dot_nn(a, b):
    return jnp.dot(a, b, preferred_element_type=F32)


def pool_kernel(par, q_ref, rk_ref, rv_ref, nk_ref, nv_ref, out_ref):
    r = pl.program_id(0)
    low, step, base, end = par[r, 0], par[r, 1], par[r, 2], par[r, 3]
    col = lax.broadcasted_iota(jnp.int32, (2 * NB, OFF + INTERVAL), 1)
    slot = lax.broadcasted_iota(jnp.int32, (2 * NB, OFF + INTERVAL), 0) % NB
    bound = jnp.minimum(base + (slot + 1) * step, end)
    allowed = (col >= low) & (col < bound)
    for pair in range(G // 2):
        q = q_ref[0, 2 * pair : 2 * pair + 2].reshape(2 * NB, HD)
        scores = jnp.concatenate([dot_nt(q, nk_ref[0]), dot_nt(q, rk_ref[0])], axis=1)
        scores = jnp.where(allowed, scores * SCALE, MASKED)
        peak = jnp.max(scores, axis=1, keepdims=True)
        weights = jnp.exp2(scores - peak)
        total = jnp.sum(weights, axis=1, keepdims=True)
        weights = weights.astype(BF)
        weighted = dot_nn(weights[:, :OFF], nv_ref[0]) + dot_nn(weights[:, OFF:], rv_ref[0])
        pooled = (weighted / total).astype(BF)
        for copy in range(4):
            for half in range(2):
                at = (2 * pair + half) * HD
                out_ref[copy, :, at : at + HD] = pooled[half * NB : (half + 1) * NB]


def pool(par, queries, raw_k, raw_v, near_k, near_v):
    return pl.pallas_call(
        pool_kernel,
        out_shape=jax.ShapeDtypeStruct((4, REQ * NB, G * HD), BF),
        grid_spec=pltpu.PrefetchScalarGridSpec(
            num_scalar_prefetch=1,
            grid=(REQ,),
            in_specs=[
                pl.BlockSpec((1, G, NB, HD), lambda r, par: (r, 0, 0, 0)),
                pl.BlockSpec((1, INTERVAL, HD), lambda r, par: (r, 0, 0)),
                pl.BlockSpec((1, INTERVAL, HD), lambda r, par: (r, 0, 0)),
                pl.BlockSpec((1, OFF, HD), lambda r, par: (r, 0, 0)),
                pl.BlockSpec((1, OFF, HD), lambda r, par: (r, 0, 0)),
            ],
            out_specs=pl.BlockSpec((4, NB, G * HD), lambda r, par: (0, r, 0)),
        ),
        compiler_params=pltpu.CompilerParams(vmem_limit_bytes=40 << 20),
        name="pool",
    )(par, queries, raw_k, raw_v, near_k, near_v)


def lanes():
    return lax.broadcasted_iota(jnp.int32, (ROWS, HD), 1)


def pieces(value):
    high = value.astype(BF).astype(F32)
    rest = value - high
    middle = rest.astype(BF).astype(F32)
    return high, middle, rest - middle


def pack(out_ref, weighted, peak, total):
    lane = lanes()
    extra = jnp.zeros((ROWS, HD), F32)
    for at, piece in enumerate(pieces(peak) + pieces(total)):
        extra = jnp.where(lane == at, piece, extra)
    weighted, extra = weighted.astype(BF), extra.astype(BF)
    for copy in range(out_ref.shape[0]):
        out_ref[copy, :, :HD] = weighted
        out_ref[copy, :, HD:] = extra


def merge(in_ref):
    lane = lanes()
    peaks, totals = [], []
    for i in range(in_ref.shape[0]):
        extra = in_ref[i, :, HD:].astype(F32)
        peaks.append(jnp.sum(jnp.where(lane < 3, extra, 0.0), axis=1, keepdims=True))
        totals.append(jnp.sum(jnp.where(lane >= 3, extra, 0.0), axis=1, keepdims=True))
    peak = peaks[0]
    for other in peaks[1:]:
        peak = jnp.maximum(peak, other)
    weighted, total = 0.0, 0.0
    for i in range(in_ref.shape[0]):
        factor = jnp.exp2(peaks[i] - peak)
        weighted += in_ref[i, :, :HD].astype(F32) * factor
        total += totals[i] * factor
    return weighted, peak, total


def decode_kernel(
    par, po_ref, pt_ref, wo_ref, wt_ref, q_ref, sk_ref, sv_ref, tk_ref, tv_ref, bk_ref, bv_ref, out_ref, acc
):
    step = pl.program_id(0)
    part = dot_nn(po_ref[0], wo_ref[...]) + dot_nn(pt_ref[0], wt_ref[...])

    @pl.when(step == 0)
    def _():
        acc[...] = part

    @pl.when(step > 0)
    def _():
        acc[...] += part

    @pl.when(step == 3)
    def _():
        queries = q_ref[...]
        of_row = lax.broadcasted_iota(jnp.int32, (ROWS, RES), 0) % REQ
        col = lax.broadcasted_iota(jnp.int32, (ROWS, RES), 1)
        row = lax.broadcasted_iota(jnp.int32, (NB, HD), 0)
        keys, values, usable = [], [], []
        for r in range(REQ):
            made = jnp.where((row < par[r, 0])[:, :1], acc[r * NB : (r + 1) * NB], 0.0).astype(BF)
            bk_ref[r] = made[:, :HD]
            bv_ref[r] = made[:, HD:]
            keys += [sk_ref[r], tk_ref[r], made[:, :HD]]
            values += [sv_ref[r], tv_ref[r], made[:, HD:]]
            mine = of_row == r
            usable += [
                mine & (col < par[r, 1]),
                mine & (col >= par[r, 2]),
                (mine & (col < par[r, 0]))[:, :NB],
            ]
        scores = [
            jnp.where(ok, dot_nt(queries, k) * SCALE, MASKED) for k, ok in zip(keys, usable)
        ]
        scores = jnp.concatenate(scores, axis=1)
        peak = jnp.max(scores, axis=1, keepdims=True)
        weights = jnp.exp2(scores - peak)
        total = jnp.sum(weights, axis=1, keepdims=True)
        weights = weights.astype(BF)
        weighted, at = 0.0, 0
        for v in values:
            weighted += dot_nn(weights[:, at : at + v.shape[0]], v)
            at += v.shape[0]
        pack(out_ref, weighted, peak, total)


def project_decode(par, p_own, p_other, weights, queries, res_k, res_v, raw_k, raw_v):
    whole = lambda i, par: (0, 0, 0)
    return pl.pallas_call(
        decode_kernel,
        out_shape=(
            jax.ShapeDtypeStruct((REQ, NB, HD), BF),
            jax.ShapeDtypeStruct((REQ, NB, HD), BF),
            jax.ShapeDtypeStruct((8, ROWS, 2 * HD), BF),
        ),
        grid_spec=pltpu.PrefetchScalarGridSpec(
            num_scalar_prefetch=1,
            grid=(4,),
            in_specs=[
                pl.BlockSpec((1, REQ * NB, G * HD), lambda i, par: (i, 0, 0)),
                pl.BlockSpec((1, REQ * NB, G * HD), lambda i, par: (i, 0, 0)),
                pl.BlockSpec((G * HD, 2 * HD), lambda i, par: (2 * i + par[2, 0], 0)),
                pl.BlockSpec((G * HD, 2 * HD), lambda i, par: (2 * i + 1 - par[2, 0], 0)),
                pl.BlockSpec((ROWS, HD), lambda i, par: (0, 0)),
                pl.BlockSpec((REQ, RES, HD), whole),
                pl.BlockSpec((REQ, RES, HD), whole),
                pl.BlockSpec((REQ, OFF, HD), lambda i, par: (0, INTERVAL // OFF - 1, 0)),
                pl.BlockSpec((REQ, OFF, HD), lambda i, par: (0, INTERVAL // OFF - 1, 0)),
            ],
            out_specs=[
                pl.BlockSpec((REQ, NB, HD), whole),
                pl.BlockSpec((REQ, NB, HD), whole),
                pl.BlockSpec((8, ROWS, 2 * HD), whole),
            ],
            scratch_shapes=[pltpu.VMEM((REQ * NB, 2 * HD), F32)],
        ),
        compiler_params=pltpu.CompilerParams(vmem_limit_bytes=40 << 20),
        name="project_decode",
    )(par, p_own, p_other, weights, weights, queries, res_k, res_v, raw_k, raw_v)


def combine_kernel(in_ref, out_ref):
    pack(out_ref, *merge(in_ref))


def combine(state):
    return pl.pallas_call(
        combine_kernel, out_shape=jax.ShapeDtypeStruct((8, ROWS, 2 * HD), BF), name="combine"
    )(state)


def attend_kernel(in_ref, w_ref, out_ref):
    weighted, _, total = merge(in_ref)
    attended = weighted / total
    rows = STEPS * REQ
    flat = jnp.concatenate([attended[g * rows : (g + 1) * rows] for g in range(G)], axis=1)
    part = dot_nn(flat.astype(BF), w_ref[...])
    for copy in range(8):
        out_ref[copy] = part


def attend(state, out_weight):
    return pl.pallas_call(
        attend_kernel,
        out_shape=jax.ShapeDtypeStruct((8, STEPS * REQ, HD), F32),
        name="attend",
    )(state, out_weight)


def body(
    raw_keys,
    raw_values,
    phase,
    ratio,
    resident_len,
    beacon_queries,
    beacon_wk,
    beacon_wv,
    resident_keys,
    resident_values,
    decode_queries,
    out_weight,
):
    shard = lax.axis_index(SEQ)
    count = lax.axis_size(SEQ)
    first, last = shard == 0, shard == count - 1
    weights = lax.all_gather(
        jnp.concatenate([beacon_wk, beacon_wv], axis=1), SEQ, axis=0, tiled=True
    )
    raw_k, raw_v = raw_keys[:, :, 0], raw_values[:, :, 0]
    tails = jnp.stack([raw_k[:, INTERVAL - OFF :], raw_v[:, INTERVAL - OFF :]])
    near = lax.ppermute(tails, SEQ, [(i, i + 1) for i in range(count - 1)])
    own_ratio = lax.dynamic_index_in_dim(ratio, shard, 1, keepdims=False)
    own_len = lax.dynamic_index_in_dim(resident_len, shard, 1, keepdims=False)
    lead = jnp.where(first, phase, 0)
    shift = OFF - phase
    pool_par = jnp.stack([lead + shift, own_ratio, lead + shift, shift + INTERVAL], axis=1)
    queries = jnp.transpose(beacon_queries[:, :, 0], (0, 2, 1, 3))
    pooled = pool(pool_par, queries, raw_k, raw_v, near[0], near[1])
    p_own = lax.all_to_all(pooled, "x", 0, 0)
    p_other = lax.ppermute(p_own, "c", [(0, 1), (1, 0)])
    live = INTERVAL // own_ratio
    leftover = jnp.where(last, shift, OFF)
    core = jnp.full((1, 3), lax.axis_index("c"), jnp.int32)
    decode_par = jnp.concatenate([jnp.stack([live, own_len, leftover], axis=1), core])
    step_queries = jnp.transpose(decode_queries[:, :, 0], (2, 0, 1, 3)).reshape(ROWS, HD)
    beacon_k, beacon_v, state = project_decode(
        decode_par,
        p_own,
        p_other,
        weights,
        step_queries,
        resident_keys[:, :, 0],
        resident_values[:, :, 0],
        raw_k,
        raw_v,
    )
    state = combine(lax.all_to_all(state, "y", 0, 0))
    parts = attend(lax.all_to_all(state, "z", 0, 0), out_weight)
    parts = lax.all_to_all(parts, ("x", "c"), 0, 0)
    projected = jnp.sum(parts, axis=0).astype(BF).reshape(STEPS, REQ, HD)
    return beacon_k[:, :, None], beacon_v[:, :, None], projected


def solution(mesh):
    fine = Mesh(mesh.devices.reshape(8, 8, 4, 2), ("z", "y", "x", "c"))
    head = ("x", "c")
    return jax.shard_map(
        body,
        mesh=fine,
        in_specs=(
            P(None, SEQ, head, None),
            P(None, SEQ, head, None),
            P(),
            P(),
            P(),
            P(None, SEQ, head, None, None),
            P(SEQ, head),
            P(SEQ, head),
            P(None, SEQ, head, None),
            P(None, SEQ, head, None),
            P(None, None, head, None, None),
            P(head, SEQ),
        ),
        out_specs=(
            P(None, SEQ, head, None),
            P(None, SEQ, head, None),
            P(None, None, SEQ),
        ),
        check_vma=False,
    )
```

time: 667 us -> 164 us (0.25)
  blocking collectives: 432 us -> 74.1 us
  waiting for transfers between devices: 184 us -> 42.9 us
  Pallas kernels: 0 us -> 15.5 us
  matrix products: 13.1 us -> 0 us
  other arithmetic: 10.8 us -> 3.11 us
    psum x2 -> x0, blocking collectives: 318 us -> none  [the longest x1 220 us: body(): lax.psum((weight_sum * rescale, weighted * rescale[..., None]), 'seq')]
    all_gather x3 -> x1, waiting for transfers between devices: 183 us -> 38.2 us  [body(): lax.all_gather(jnp.concatenate([beacon_wk, beacon_wv], axis=1), SEQ, axis...]
    pmax x1 -> x0, blocking collectives: 113 us -> none  [body(): global_peak = lax.pmax(row_peak, 'seq')]
    all_to_all x0 -> x4, blocking collectives: none -> 74.1 us  [the longest x1 30.1 us: body(): p_own = lax.all_to_all(pooled, 'x', 0, 0)]
    pallas_call x0 -> x4, Pallas kernels: none -> 15.5 us  [the longest x1 6.27 us: pool(): pl.pallas_call(pool_kernel, out_shape=jax.ShapeDtypeStruct((4, REQ * NB,...]
    dot_general x9 -> x0, matrix products: 13.1 us -> none  [the longest x1 4.11 us: body(): jnp.dot(pooled_whole, lax.all_gather(beacon_wk, 'seq', axis=0, tiled=True...]
  transfers between devices with their start and end apart: 5 -> 3, of which waited for: 3 -> 3; matrix products, arithmetic and copies ran while one was open for 3% -> 2% of each run, Pallas kernels for 0% -> 4%
where the time goes in v1:
time: 164 us; the launch traced here: 163 us
  blocking collectives  74.1 us (45%)
  waiting for transfers between devices  42.9 us (26%)
  Pallas kernels  15.5 us (9%)
  between operations  14.2 us (9%)
  starting transfers between devices  8.74 us (5%)
  local copies, waits for them, and re-layouts  4.67 us (3%)
  other arithmetic  3.11 us (2%)
    all_gather x1, waiting for transfers between devices, body(): lax.all_gather(jnp.concatenate([beacon_wk, beacon_wv], axis=1), SEQ, axis...  38.2 us
    all_to_all x1, blocking collectives, body(): p_own = lax.all_to_all(pooled, 'x', 0, 0)  30.1 us
    all_to_all x1, blocking collectives, body(): parts = lax.all_to_all(parts, ('x', 'c'), 0, 0)  15.9 us
    all_to_all x1, blocking collectives, body(): parts = attend(lax.all_to_all(state, 'z', 0, 0), out_weight)  14.1 us
    all_to_all x1, blocking collectives, body(): state = combine(lax.all_to_all(state, 'y', 0, 0))  14 us
    pallas_call x1, Pallas kernels, pool(): pl.pallas_call(pool_kernel, out_shape=jax.ShapeDtypeStruct((4, REQ * NB,...  6.27 us
    pallas_call x1, Pallas kernels, project_decode(): pl.pallas_call(decode_kernel, out_shape=(jax.ShapeDtypeStruct((REQ, NB, H...  5.31 us
    ppermute x1, starting transfers between devices, body(): p_other = lax.ppermute(p_own, 'c', [(0, 1), (1, 0)])  4.66 us
  transfers between devices with their start and end apart: 3, of which 3 were waited for; matrix products, arithmetic and copies ran while one was open for 2% of the time, Pallas kernels for 4%

profile of v1, /device:TPU:1, one launch (start us, length us, event | category | flops | bytes accessed | tf_op | source)
XLA Modules:
  0.0 163.3 jit_solution(18009818492957843149)
XLA Ops:
  7.2 0.0 copy-start.2
  7.2 0.0 copy-start.1
  7.2 0.0 all-gather.2.cloned.1.call-start
  7.3 1.5 pad_maximum_fusion.1
  8.7 0.0 all-gather.2.cloned.1.call-update
  8.8 1.0 slice_bitcast_fusion.2
  9.8 4.0 %collective-permute-start = (bf16[2,2,256,128]{3,2,1,0:T(8,128)(2,1)S(1)}, bf16[2,2,256,128]{3,2,1,0:T(8,128)(2,1)S(1)}, u32[]{:S(2)}, u32[]{:S(2)}) collective-permute-start(bf16[2,2,256,128]{3,2,1,0:T(8,128)(2,1)S(1)} %pad_maximum_fusion), channel_id=1, source_target_pairs={{0,8},{8,16},{16,24},{24,32},{32,40},{40,48},{48,56},{56,64},{64,7... | collective-permute-start | bytes 786440 | tf_op jit(solution)/shard_map/ppermute | solution.py:251
  13.9 0.7 fusion.2
  14.5 0.1 copy.16
  14.6 0.1 copy.18
  14.7 1.1 copy.24
  15.9 0.2 and_select_fusion
  16.1 0.1 pad_add_fusion.1.par
  16.2 1.0 collective-permute-done
  17.2 6.3 %pool.1 = bf16[4,256,1024]{2,1,0:T(8,128)(2,1)S(1)} custom-call(s32[2,4]{1,0:T(2,128)S(1)} %pad_add_fusion.1.par, bf16[2,8,128,128]{3,2,1,0:T(8,128)(2,1)S(1)} %bitcast.40, bf16[2,1024,128]{2,1,0:T(8,128)(2,1)S(1)} %bitcast.35, bf16[2,1024,128]{2,1,0:T(8,128)(2,1)S(1)} %bitcast.38, bf16[2,256,128]{2,1,0:T(8,128)(2,1)S(1)} %get-tuple-element.15.nk_ref, ...), custom_call_target="tpu_custom_call" | custom-call | tf_op jit(solution)/shard_map/pool/pallas_call | solution.py:58
  23.5 0.0 copy-start.5
  23.5 0.0 copy-start.3
  23.5 0.0 copy-start.4
  23.5 30.1 %all_to_all.20.po_ref = bf16[4,256,1024]{2,1,0:T(8,128)(2,1)S(1)} all-to-all(bf16[4,256,1024]{2,1,0:T(8,128)(2,1)S(1)} %pool.1), channel_id=1, replica_groups=mesh['z'=8,'y'=8,'x'=4,'c'=2] {'x'}, dimensions={0} | all-to-all | bytes 4194304 | tf_op jit(solution)/shard_map/all_to_all | solution.py:259
  53.6 4.7 %collective-permute-start.1 = (bf16[4,256,1024]{2,1,0:T(8,128)(2,1)S(1)}, bf16[4,256,1024]{2,1,0:T(8,128)(2,1)}, u32[]{:S(2)}, u32[]{:S(2)}) collective-permute-start(bf16[4,256,1024]{2,1,0:T(8,128)(2,1)S(1)} %all_to_all.20.po_ref), channel_id=1, source_target_pairs={{0,1},{1,0},{2,3},{3,2},{4,5},{5,4},{6,7},{7,6},{8,9},{9,8},{10,11... | collective-permute-start | bytes 6291464 | tf_op jit(solution)/shard_map/ppermute | solution.py:260
  58.3 0.1 copy.15
  58.4 0.1 pad_add_fusion
  58.5 3.7 %collective-permute-done.1.pt_ref = bf16[4,256,1024]{2,1,0:T(8,128)(2,1)} collective-permute-done((bf16[4,256,1024]{2,1,0:T(8,128)(2,1)S(1)}, bf16[4,256,1024]{2,1,0:T(8,128)(2,1)}, u32[]{:S(2)}, u32[]{:S(2)}) %collective-permute-start.1) | collective-permute-done | bytes 2097184 | tf_op jit(solution)/shard_map/ppermute | solution.py:260
  62.2 38.2 %all-gather.2.cloned.1.call-done.wo_ref.wt_ref = bf16[8192,256]{1,0:T(8,128)(2,1)} async-done(((bf16[128,256]{1,0:T(8,128)(2,1)}), bf16[8192,256]{1,0:T(8,128)(2,1)}) %all-gather.2.cloned.1.call-update) | async-done | bytes 4194320 | tf_op jit(solution)/shard_map/all_gather | solution.py:246
  100.4 2.2 %copy-done = bf16[8192,256]{1,0:T(8,128)(2,1)S(1)} copy-done((bf16[8192,256]{1,0:T(8,128)(2,1)S(1)}, bf16[8192,256]{1,0:T(8,128)(2,1)}, u32[]{:S(2)}) %copy-start) | copy-done | bytes 4194328
  102.6 5.3 %project_decode.1 = (bf16[2,128,128]{2,1,0:T(8,128)(2,1)}, bf16[2,128,128]{2,1,0:T(8,128)(2,1)}, bf16[8,64,256]{2,1,0:T(8,128)(2,1)S(1)}) custom-call(s32[3,3]{1,0:T(4,128)S(1)} %concatenate.6.par, bf16[4,256,1024]{2,1,0:T(8,128)(2,1)S(1)} %all_to_all.20.po_ref, bf16[4,256,1024]{2,1,0:T(8,128)(2,1)} %collective-permute-done.1.pt_ref, ...), custom_call_target="tpu_custom_call" | custom-call | tf_op jit(solution)/shard_map/project_decode/pallas_call | solution.py:168
  107.9 14.0 %all_to_all.21.in_ref = bf16[8,64,256]{2,1,0:T(8,128)(2,1)} all-to-all(bf16[8,64,256]{2,1,0:T(8,128)(2,1)S(1)} %get-tuple-element.8), channel_id=1, replica_groups=mesh['z'=8,'y'=8,'x'=4,'c'=2] {'y'}, dimensions={0} | all-to-all | bytes 524288 | tf_op jit(solution)/shard_map/all_to_all | solution.py:277
  121.9 1.9 %combine.1 = bf16[8,64,256]{2,1,0:T(8,128)(2,1)} custom-call(bf16[8,64,256]{2,1,0:T(8,128)(2,1)} %all_to_all.21.in_ref), custom_call_target="tpu_custom_call" | custom-call | tf_op jit(solution)/shard_map/combine/pallas_call | solution.py:206
  123.8 14.1 %all_to_all.22.in_ref = bf16[8,64,256]{2,1,0:T(8,128)(2,1)} all-to-all(bf16[8,64,256]{2,1,0:T(8,128)(2,1)} %combine.1), channel_id=1, replica_groups=mesh['z'=8,'y'=8,'x'=4,'c'=2] {'z'}, dimensions={0} | all-to-all | bytes 524288 | tf_op jit(solution)/shard_map/all_to_all | solution.py:278
  137.9 2.0 %attend.1 = f32[8,8,128]{2,1,0:T(8,128)} custom-call(bf16[8,64,256]{2,1,0:T(8,128)(2,1)} %all_to_all.22.in_ref, bf16[1024,128]{1,0:T(8,128)(2,1)} %w_ref.1), custom_call_target="tpu_custom_call" | custom-call | tf_op jit(solution)/shard_map/attend/pallas_call | solution.py:222
  139.9 15.9 %all_to_all.23 = f32[8,8,128]{2,1,0:T(8,128)S(1)} all-to-all(f32[8,8,128]{2,1,0:T(8,128)} %attend.1), channel_id=1, replica_groups=mesh['z'=8,'y'=8,'x'=4,'c'=2] {'x','c'}, dimensions={0} | all-to-all | bytes 65536 | tf_op jit(solution)/shard_map/all_to_all | solution.py:279
  155.8 0.6 reduce_sum.9
  (14 shorter events, 0.1 us)
Async XLA Ops:
  7.2 10.0 %copy-start.2 = (bf16[2,1024,1,128]{3,1,2,0:T(8,128)(2,1)S(1)}, bf16[2,1024,1,128]{3,1,2,0:T(8,128)(2,1)}, u32[]{:S(2)}) copy-start(bf16[2,1024,1,128]{3,1,2,0:T(8,128)(2,1)} %param.13) | copy-start | bytes 1572868
  7.2 10.0 %copy-start.1 = (bf16[2,1024,1,128]{3,1,2,0:T(8,128)(2,1)S(1)}, bf16[2,1024,1,128]{3,1,2,0:T(8,128)(2,1)}, u32[]{:S(2)}) copy-start(bf16[2,1024,1,128]{3,1,2,0:T(8,128)(2,1)} %param.12) | copy-start | bytes 1572868
  7.2 8.7 %copy-start.7 = (s32[2,64]{1,0:T(2,128)S(1)}, s32[2,64]{1,0:T(2,128)}, u32[]{:S(2)}) copy-start(s32[2,64]{1,0:T(2,128)} %param.16) | copy-start | bytes 1540
  7.2 8.7 %copy-start.6 = (s32[2,64]{1,0:T(2,128)S(1)}, s32[2,64]{1,0:T(2,128)}, u32[]{:S(2)}) copy-start(s32[2,64]{1,0:T(2,128)} %param.15) | copy-start | bytes 1540
  7.2 93.2 %all-gather.2.cloned.1.call-start = ((), (), s32[]{:S(2)}) async-start(), calls=%async_computation.4 | async-start | bytes 4259840 | tf_op jit(solution)/shard_map/all_gather | solution.py:246
  9.8 7.3 %collective-permute-start = (bf16[2,2,256,128]{3,2,1,0:T(8,128)(2,1)S(1)}, bf16[2,2,256,128]{3,2,1,0:T(8,128)(2,1)S(1)}, u32[]{:S(2)}, u32[]{:S(2)}) collective-permute-start(bf16[2,2,256,128]{3,2,1,0:T(8,128)(2,1)S(1)} %pad_maximum_fusion), channel_id=1, source_target_pairs={{0,8},{8,16},{16,24},{24,32},{32,40},{40,48},{48,56},{56,64},{64,7... | collective-permute-start | bytes 786440 | tf_op jit(solution)/shard_map/ppermute | solution.py:251
  23.5 34.9 %copy-start.5 = (bf16[4,2,1,8,128]{4,3,2,1,0:T(8,128)(2,1)S(1)}, bf16[4,2,1,8,128]{4,3,2,1,0:T(8,128)(2,1)}, u32[]{:S(2)}) copy-start(bf16[4,2,1,8,128]{4,3,2,1,0:T(8,128)(2,1)} %param.22) | copy-start | bytes 49156
  23.5 77.0 %copy-start.3 = (bf16[2,256,1,128]{3,1,2,0:T(8,128)(2,1)S(1)}, bf16[2,256,1,128]{3,1,2,0:T(8,128)(2,1)}, u32[]{:S(2)}) copy-start(bf16[2,256,1,128]{3,1,2,0:T(8,128)(2,1)} %param.20) | copy-start | bytes 393220
  23.5 77.0 %copy-start.4 = (bf16[2,256,1,128]{3,1,2,0:T(8,128)(2,1)S(1)}, bf16[2,256,1,128]{3,1,2,0:T(8,128)(2,1)}, u32[]{:S(2)}) copy-start(bf16[2,256,1,128]{3,1,2,0:T(8,128)(2,1)} %param.21) | copy-start | bytes 393220
  53.6 8.6 %collective-permute-start.1 = (bf16[4,256,1024]{2,1,0:T(8,128)(2,1)S(1)}, bf16[4,256,1024]{2,1,0:T(8,128)(2,1)}, u32[]{:S(2)}, u32[]{:S(2)}) collective-permute-start(bf16[4,256,1024]{2,1,0:T(8,128)(2,1)S(1)} %all_to_all.20.po_ref), channel_id=1, source_target_pairs={{0,1},{1,0},{2,3},{3,2},{4,5},{5,4},{6,7},{7,6},{8,9},{9,8},{10,11... | collective-permute-start | bytes 6291464 | tf_op jit(solution)/shard_map/ppermute | solution.py:260
  100.4 2.2 %copy-start = (bf16[8192,256]{1,0:T(8,128)(2,1)S(1)}, bf16[8192,256]{1,0:T(8,128)(2,1)}, u32[]{:S(2)}) copy-start(bf16[8192,256]{1,0:T(8,128)(2,1)} %all-gather.2.cloned.1.call-done.wo_ref.wt_ref) | copy-start | bytes 12582916
Sparse Core Ops, SparseCore 0:
  11.7 88.7 all-gather.1

commit v2 on v1

v2 whole, which is shorter than its diff:
```python
import math

import jax
import jax.numpy as jnp
from jax import lax
from jax.experimental import pallas as pl
from jax.experimental.pallas import tpu as pltpu
from jax.sharding import Mesh, PartitionSpec as P

G = 8
HD = 128
INTERVAL = 1024
NB = 128
OFF = 256
STEPS = 4
REQ = 2
RES = 256
ROWS = STEPS * REQ * G
SCALE = math.log2(math.e) / math.sqrt(HD)
MASKED = -1e30
SEQ = ("z", "y")
BF = jnp.bfloat16
F32 = jnp.float32


def dot_nt(a, b):
    return lax.dot_general(a, b, (((1,), (1,)), ((), ())), preferred_element_type=F32)


def dot_nn(a, b):
    return jnp.dot(a, b, preferred_element_type=F32)


def stage_kernel(wk_ref, wv_ref, tk_ref, tv_ref, w_ref, tails_ref):
    for copy in range(8):
        w_ref[copy, :, :HD] = wk_ref[...]
        w_ref[copy, :, HD:] = wv_ref[...]
    tails_ref[0] = tk_ref[...]
    tails_ref[1] = tv_ref[...]


def stage(wk, wv, raw_k, raw_v):
    tail = pl.BlockSpec((REQ, OFF, HD), lambda i: (0, INTERVAL // OFF - 1, 0))
    weight = pl.BlockSpec((HD, HD), lambda i: (0, 0))
    return pl.pallas_call(
        stage_kernel,
        out_shape=(
            jax.ShapeDtypeStruct((8, HD, 2 * HD), BF),
            jax.ShapeDtypeStruct((2, REQ, OFF, HD), BF),
        ),
        grid=(1,),
        in_specs=[weight, weight, tail, tail],
        out_specs=(
            pl.BlockSpec((8, HD, 2 * HD), lambda i: (0, 0, 0)),
            pl.BlockSpec((2, REQ, OFF, HD), lambda i: (0, 0, 0, 0)),
        ),
        name="stage",
    )(wk, wv, raw_k, raw_v)


def pool_kernel(at_ref, phase_ref, ratio_ref, q_ref, rk_ref, rv_ref, near_ref, out_ref):
    r = pl.program_id(0)
    shard = at_ref[0]
    phase, step = phase_ref[r], ratio_ref[r, shard]
    start = OFF - phase
    low = start + jnp.where(shard == 0, phase, 0)
    col = lax.broadcasted_iota(jnp.int32, (2 * NB, OFF + INTERVAL), 1)
    slot = lax.broadcasted_iota(jnp.int32, (2 * NB, OFF + INTERVAL), 0) % NB
    bound = jnp.minimum(low + (slot + 1) * step, start + INTERVAL)
    allowed = (col >= low) & (col < bound)
    for pair in range(G // 2):
        q = q_ref[0, 2 * pair : 2 * pair + 2].reshape(2 * NB, HD)
        scores = jnp.concatenate([dot_nt(q, near_ref[0, 0]), dot_nt(q, rk_ref[0])], axis=1)
        scores = jnp.where(allowed, scores * SCALE, MASKED)
        peak = jnp.max(scores, axis=1, keepdims=True)
        weights = jnp.exp2(scores - peak)
        total = jnp.sum(weights, axis=1, keepdims=True)
        weights = weights.astype(BF)
        weighted = dot_nn(weights[:, :OFF], near_ref[1, 0]) + dot_nn(weights[:, OFF:], rv_ref[0])
        pooled = (weighted / total).astype(BF)
        for copy in range(4):
            for half in range(2):
                at = (2 * pair + half) * HD
                out_ref[copy, :, at : at + HD] = pooled[half * NB : (half + 1) * NB]


def pool(at, phase, ratio, queries, raw_k, raw_v, near):
    return pl.pallas_call(
        pool_kernel,
        out_shape=jax.ShapeDtypeStruct((4, REQ * NB, G * HD), BF),
        grid_spec=pltpu.PrefetchScalarGridSpec(
            num_scalar_prefetch=3,
            grid=(REQ,),
            in_specs=[
                pl.BlockSpec((1, G, NB, HD), lambda r, *_: (r, 0, 0, 0)),
                pl.BlockSpec((1, INTERVAL, HD), lambda r, *_: (r, 0, 0)),
                pl.BlockSpec((1, INTERVAL, HD), lambda r, *_: (r, 0, 0)),
                pl.BlockSpec((2, 1, OFF, HD), lambda r, *_: (0, r, 0, 0)),
            ],
            out_specs=pl.BlockSpec((4, NB, G * HD), lambda r, *_: (0, r, 0)),
        ),
        compiler_params=pltpu.CompilerParams(vmem_limit_bytes=40 << 20),
        name="pool",
    )(at, phase, ratio, queries, raw_k, raw_v, near)


def pieces(value):
    high = value.astype(BF).astype(F32)
    rest = value - high
    middle = rest.astype(BF).astype(F32)
    return high, middle, rest - middle


def pack(out_ref, weighted, peak, total):
    row = lax.broadcasted_iota(jnp.int32, (16, HD), 0)
    extra = jnp.zeros((16, HD), F32)
    for at, piece in enumerate(pieces(peak) + pieces(total)):
        extra = jnp.where(row == at, piece, extra)
    weighted, extra = weighted.astype(BF), extra.astype(BF)
    for copy in range(out_ref.shape[0]):
        out_ref[copy, :ROWS] = weighted
        out_ref[copy, ROWS:] = extra


def merge(in_ref, divide):
    extra = in_ref[:, ROWS:, :].astype(F32)
    peaks = extra[:, 0] + extra[:, 1] + extra[:, 2]
    totals = extra[:, 3] + extra[:, 4] + extra[:, 5]
    peak = jnp.max(peaks, axis=0, keepdims=True)
    factors = jnp.exp2(peaks - peak)
    total = jnp.sum(totals * factors, axis=0, keepdims=True)
    scales = (factors / total if divide else factors).T
    weighted = 0.0
    for i in range(in_ref.shape[0]):
        weighted += in_ref[i, :ROWS].astype(F32) * scales[:ROWS, i : i + 1]
    return weighted, peak, total


def decode_kernel(
    at_ref, phase_ref, ratio_ref, len_ref,
    po_ref, pt_ref, w_ref, q_ref, sk_ref, sv_ref, rk_ref, rv_ref,
    bk_ref, bv_ref, out_ref, held, other, sems, other_sems,
):
    shard, core, last = at_ref[0], at_ref[1], at_ref[2]
    copies = [
        pltpu.make_async_copy(w_ref.at[pl.ds(k * G * HD, G * HD)], held.at[k], sems.at[k])
        for k in range(8)
    ]
    other_copies = [
        pltpu.make_async_copy(pt_ref.at[x], other.at[x], other_sems.at[x]) for x in range(4)
    ]
    for x in range(4):
        copies[2 * x].start()
        copies[2 * x + 1].start()
        other_copies[x].start()
    queries = q_ref[...]
    of_row = lax.broadcasted_iota(jnp.int32, (ROWS, RES), 0) % REQ
    col = lax.broadcasted_iota(jnp.int32, (ROWS, RES), 1)
    row = lax.broadcasted_iota(jnp.int32, (NB, 2 * HD), 0)
    live = [INTERVAL // ratio_ref[r, shard] for r in range(REQ)]

    def score(keys, usable):
        return jnp.where(usable, dot_nt(queries, keys) * SCALE, MASKED)

    early, late = [], []
    for r in range(REQ):
        mine = of_row == r
        leftover = jnp.where(last == 1, OFF - phase_ref[r], OFF)
        early.append(score(sk_ref[r], mine & (col < len_ref[r, shard])))
        early.append(score(rk_ref[r], mine & (col >= leftover)))
    total_part = 0.0
    for x in range(4):
        copies[2 * x].wait()
        copies[2 * x + 1].wait()
        other_copies[x].wait()
        total_part += dot_nn(po_ref[x], held[2 * x + core])
        total_part += dot_nn(other[x], held[2 * x + 1 - core])
    made = []
    for r in range(REQ):
        part = total_part[r * NB : (r + 1) * NB]
        made.append(jnp.where(row < live[r], part, 0.0).astype(BF))
        bk_ref[r] = made[r][:, :HD]
        bv_ref[r] = made[r][:, HD:]
        late.append(score(made[r][:, :HD], (of_row == r)[:, :NB] & (col[:, :NB] < live[r])))
    scores = jnp.concatenate(early + late, axis=1)
    peak = jnp.max(scores, axis=1, keepdims=True)
    weights = jnp.exp2(scores - peak)
    total = jnp.sum(weights, axis=1, keepdims=True)
    weights = weights.astype(BF)
    values = [sv_ref[0], rv_ref[0], sv_ref[1], rv_ref[1], made[0][:, HD:], made[1][:, HD:]]
    weighted, at = 0.0, 0
    for v in values:
        weighted += dot_nn(weights[:, at : at + v.shape[0]], v)
        at += v.shape[0]
    lane = lax.broadcasted_iota(jnp.int32, (ROWS, HD), 1)
    columns = jnp.where(lane == 0, peak, total)
    rows = jnp.concatenate([columns, jnp.zeros((HD - ROWS, HD), F32)], axis=0).T
    pack(out_ref, weighted, rows[0:1], rows[1:2])


def project_decode(at, phase, ratio, length, p_own, p_other, weights, queries, res_k, res_v, raw_k, raw_v):
    whole = lambda i, *_: (0, 0, 0)
    tail = pl.BlockSpec((REQ, OFF, HD), lambda i, *_: (0, INTERVAL // OFF - 1, 0))
    return pl.pallas_call(
        decode_kernel,
        out_shape=(
            jax.ShapeDtypeStruct((REQ, NB, HD), BF),
            jax.ShapeDtypeStruct((REQ, NB, HD), BF),
            jax.ShapeDtypeStruct((8, ROWS + 16, HD), BF),
        ),
        grid_spec=pltpu.PrefetchScalarGridSpec(
            num_scalar_prefetch=4,
            grid=(1,),
            in_specs=[
                pl.BlockSpec((4, REQ * NB, G * HD), whole),
                pl.BlockSpec(memory_space=pltpu.HBM),
                pl.BlockSpec(memory_space=pltpu.HBM),
                pl.BlockSpec((ROWS, HD), lambda i, *_: (0, 0)),
                pl.BlockSpec((REQ, RES, HD), whole),
                pl.BlockSpec((REQ, RES, HD), whole),
                tail,
                tail,
            ],
            out_specs=[
                pl.BlockSpec((REQ, NB, HD), whole),
                pl.BlockSpec((REQ, NB, HD), whole),
                pl.BlockSpec((8, ROWS + 16, HD), whole),
            ],
            scratch_shapes=[
                pltpu.VMEM((8, G * HD, 2 * HD), BF),
                pltpu.VMEM((4, REQ * NB, G * HD), BF),
                pltpu.SemaphoreType.DMA((8,)),
                pltpu.SemaphoreType.DMA((4,)),
            ],
        ),
        compiler_params=pltpu.CompilerParams(vmem_limit_bytes=40 << 20),
        name="project_decode",
    )(
        at,
        phase,
        ratio,
        length,
        p_own,
        pltpu.with_memory_space_constraint(p_other, pltpu.HBM),
        pltpu.with_memory_space_constraint(weights, pltpu.HBM),
        queries,
        res_k,
        res_v,
        raw_k,
        raw_v,
    )


def combine_kernel(in_ref, out_ref):
    pack(out_ref, *merge(in_ref, False))


def combine(state):
    return pl.pallas_call(
        combine_kernel, out_shape=pltpu.VMEM(state.shape, BF), name="combine"
    )(pltpu.with_memory_space_constraint(state, pltpu.VMEM))


def attend_kernel(in_ref, w_ref, out_ref):
    attended, _, _ = merge(in_ref, True)
    rows = STEPS * REQ
    flat = jnp.concatenate([attended[g * rows : (g + 1) * rows] for g in range(G)], axis=1)
    part = dot_nn(flat.astype(BF), w_ref[...])
    for copy in range(8):
        out_ref[copy] = part


def attend(state, out_weight):
    return pl.pallas_call(
        attend_kernel,
        out_shape=pltpu.VMEM((8, STEPS * REQ, HD), F32),
        name="attend",
    )(pltpu.with_memory_space_constraint(state, pltpu.VMEM), out_weight)


def body(
    raw_keys,
    raw_values,
    phase,
    ratio,
    resident_len,
    beacon_queries,
    beacon_wk,
    beacon_wv,
    resident_keys,
    resident_values,
    decode_queries,
    out_weight,
):
    shard = lax.axis_index(SEQ)
    count = lax.axis_size(SEQ)
    raw_k, raw_v = raw_keys[:, :, 0], raw_values[:, :, 0]
    staged, tails = stage(beacon_wk, beacon_wv, raw_k, raw_v)
    near = lax.ppermute(tails, SEQ, [(i, i + 1) for i in range(count - 1)])
    column = lax.all_to_all(staged, "y", 0, 0).reshape(8 * HD, 2 * HD)
    weights = lax.all_gather(column, "z", axis=0, tiled=True)
    at = jnp.stack([shard, lax.axis_index("c"), (shard == count - 1).astype(jnp.int32)])
    queries = jnp.transpose(beacon_queries[:, :, 0], (0, 2, 1, 3))
    pooled = pool(at, phase, ratio, queries, raw_k, raw_v, near)
    p_own = lax.all_to_all(pooled, "x", 0, 0)
    p_other = lax.ppermute(p_own, "c", [(0, 1), (1, 0)])
    step_queries = jnp.transpose(decode_queries[:, :, 0], (2, 0, 1, 3)).reshape(ROWS, HD)
    beacon_k, beacon_v, state = project_decode(
        at,
        phase,
        ratio,
        resident_len,
        p_own,
        p_other,
        weights,
        step_queries,
        resident_keys[:, :, 0],
        resident_values[:, :, 0],
        raw_k,
        raw_v,
    )
    state = combine(lax.all_to_all(state, "y", 0, 0))
    parts = attend(lax.all_to_all(state, "z", 0, 0), out_weight)
    parts = lax.all_to_all(parts, ("x", "c"), 0, 0)
    projected = jnp.sum(parts, axis=0).astype(BF).reshape(STEPS, REQ, HD)
    return beacon_k[:, :, None], beacon_v[:, :, None], projected


def solution(mesh):
    fine = Mesh(mesh.devices.reshape(8, 8, 4, 2), ("z", "y", "x", "c"))
    head = ("x", "c")
    return jax.shard_map(
        body,
        mesh=fine,
        in_specs=(
            P(None, SEQ, head, None),
            P(None, SEQ, head, None),
            P(),
            P(),
            P(),
            P(None, SEQ, head, None, None),
            P(SEQ, head),
            P(SEQ, head),
            P(None, SEQ, head, None),
            P(None, SEQ, head, None),
            P(None, None, head, None, None),
            P(head, SEQ),
        ),
        out_specs=(
            P(None, SEQ, head, None),
            P(None, SEQ, head, None),
            P(None, None, SEQ),
        ),
        check_vma=False,
    )
```

time: 164 us -> 147 us (0.90)
  waiting for transfers between devices: 42.9 us -> 18.2 us
  blocking collectives: 74.1 us -> 88.9 us
  local copies, waits for them, and re-layouts: 4.67 us -> 0.15 us
  other arithmetic: 3.11 us -> 0.67 us
    all_gather x1, waiting for transfers between devices: 38.2 us -> 10.9 us  [body(): weights = lax.all_gather(column, 'z', axis=0, tiled=True)]
    all_to_all x0 -> x1, blocking collectives: none -> 21.1 us  [body(): column = lax.all_to_all(staged, 'y', 0, 0).reshape(8 * HD, 2 * HD)]
    all_to_all x1, blocking collectives: 15.9 us -> 12.7 us  [body(): parts = lax.all_to_all(parts, ('x', 'c'), 0, 0)]
    unnamed x17 -> x19, local copies, waits for them, and re-layouts: 3.36 us -> 0.14 us
    ppermute x1, starting transfers between devices: 4.05 us -> 1.45 us  [body(): near = lax.ppermute(tails, SEQ, [(i, i + 1) for i in range(count - 1)])]
    ppermute x1, starting transfers between devices: 4.66 us -> 7.24 us  [body(): p_other = lax.ppermute(p_own, 'c', [(0, 1), (1, 0)])]
    ppermute x1, waiting for transfers between devices: 0.99 us -> 3.4 us  [body(): near = lax.ppermute(tails, SEQ, [(i, i + 1) for i in range(count - 1)])]
    all_to_all x1, blocking collectives: 14.1 us -> 12 us  [body(): parts = attend(lax.all_to_all(state, 'z', 0, 0), out_weight)]
  transfers between devices with their start and end apart: 3 -> 3, of which waited for: 3 -> 3; matrix products, arithmetic and copies ran while one was open for 2% -> 0% of each run, Pallas kernels for 4% -> 4%
where the time goes in v2:
time: 147 us
  blocking collectives  88.9 us (60%)
  waiting for transfers between devices  18.2 us (12%)
  Pallas kernels  15.8 us (11%)
  between operations  14.2 us (10%)
  starting transfers between devices  8.73 us (6%)
    all_to_all x1, blocking collectives, body(): p_own = lax.all_to_all(pooled, 'x', 0, 0)  28.7 us
    all_to_all x1, blocking collectives, body(): column = lax.all_to_all(staged, 'y', 0, 0).reshape(8 * HD, 2 * HD)  21.1 us
    all_to_all x1, blocking collectives, body(): state = combine(lax.all_to_all(state, 'y', 0, 0))  14.4 us
    all_to_all x1, blocking collectives, body(): parts = lax.all_to_all(parts, ('x', 'c'), 0, 0)  12.7 us
    all_to_all x1, blocking collectives, body(): parts = attend(lax.all_to_all(state, 'z', 0, 0), out_weight)  12 us
    all_gather x1, waiting for transfers between devices, body(): weights = lax.all_gather(column, 'z', axis=0, tiled=True)  10.9 us
    ppermute x1, starting transfers between devices, body(): p_other = lax.ppermute(p_own, 'c', [(0, 1), (1, 0)])  7.24 us
    pallas_call x1, Pallas kernels, pool(): pl.pallas_call(pool_kernel, out_shape=jax.ShapeDtypeStruct((4, REQ * NB,...  6.37 us
  transfers between devices with their start and end apart: 3, of which 3 were waited for; matrix products, arithmetic and copies ran while one was open for 0% of the time, Pallas kernels for 4%

profile of v2, /device:TPU:1, one launch (start us, length us, event | category | flops | bytes accessed | tf_op | source)
XLA Modules:
  0.0 146.6 jit_solution(3219006465883111898)
XLA Ops:
  7.2 0.0 copy-start.1
  7.2 0.0 copy-start
  7.2 0.0 copy-start.7
  7.2 0.0 copy-start.4
  7.2 0.0 copy-start.5
  7.2 0.0 all-gather.2.cloned.1.call-start
  7.3 2.1 %stage.1 = (bf16[8,128,256]{2,1,0:T(8,128)(2,1)}, bf16[2,2,256,128]{3,2,1,0:T(8,128)(2,1)}) custom-call(bf16[128,128]{1,0:T(8,128)(2,1)} %wk_ref.1, bf16[128,128]{1,0:T(8,128)(2,1)} %wv_ref.1, bf16[2,1024,128]{2,1,0:T(8,128)(2,1)} %bitcast.24, bf16[2,1024,128]{2,1,0:T(8,128)(2,1)} %bitcast.27), custom_call_target="tpu_custom_call" | custom-call | tf_op jit(solution)/shard_map/stage/pallas_call | solution.py:45
  9.3 21.1 %all_to_all.25 = bf16[8,128,256]{2,1,0:T(8,128)(2,1)} all-to-all(bf16[8,128,256]{2,1,0:T(8,128)(2,1)} %get-tuple-element.9), channel_id=1, replica_groups=mesh['z'=8,'y'=8,'x'=4,'c'=2] {'y'}, dimensions={0} | all-to-all | bytes 1048576 | tf_op jit(solution)/shard_map/all_to_all | solution.py:300
  30.4 0.0 all-gather.2.cloned.1.call-update
  30.5 1.4 collective-permute-start
  31.9 0.0 copy-done.7
  31.9 0.1 copy.20
  32.0 0.1 pad_add_fusion.at_ref
  32.1 3.4 %collective-permute-done.near_ref = bf16[2,2,256,128]{3,2,1,0:T(8,128)(2,1)S(1)} collective-permute-done((bf16[2,2,256,128]{3,2,1,0:T(8,128)(2,1)}, bf16[2,2,256,128]{3,2,1,0:T(8,128)(2,1)S(1)}, u32[]{:S(2)}, u32[]{:S(2)}) %collective-permute-start) | collective-permute-done | bytes 262176 | tf_op jit(solution)/shard_map/ppermute | solution.py:299
  35.5 0.0 copy-done.1
  35.5 0.0 copy-done.4
  35.5 6.4 %pool.1 = bf16[4,256,1024]{2,1,0:T(8,128)(2,1)S(1)} custom-call(s32[3]{0:T(128)S(1)} %pad_add_fusion.at_ref, s32[2]{0:T(128)S(1)} %copy-done.5, s32[2,64]{1,0:T(2,128)S(1)} %copy-done.4, bf16[2,8,128,128]{3,2,1,0:T(8,128)(2,1)S(1)} %bitcast.30, bf16[2,1024,128]{2,1,0:T(8,128)(2,1)S(1)} %bitcast.25, bf16[2,1024,128]{2,1,0:T(8,128)(2,1)S(1)} %bitcast.28, ...), custom_call_target="tpu_custom_call" | custom-call | tf_op jit(solution)/shard_map/pool/pallas_call | solution.py:88
  41.9 0.0 copy-start.8
  41.9 0.0 copy-start.2
  41.9 0.0 copy-start.3
  41.9 0.0 copy-start.6
  42.0 28.7 %all_to_all.26.po_ref = bf16[4,256,1024]{2,1,0:T(8,128)(2,1)S(1)} all-to-all(bf16[4,256,1024]{2,1,0:T(8,128)(2,1)S(1)} %pool.1), channel_id=1, replica_groups=mesh['z'=8,'y'=8,'x'=4,'c'=2] {'x'}, dimensions={0} | all-to-all | bytes 4194304 | tf_op jit(solution)/shard_map/all_to_all | solution.py:305
  70.7 7.2 %collective-permute-start.1 = (bf16[4,256,1024]{2,1,0:T(8,128)(2,1)S(1)}, bf16[4,256,1024]{2,1,0:T(8,128)(2,1)}, u32[]{:S(2)}, u32[]{:S(2)}) collective-permute-start(bf16[4,256,1024]{2,1,0:T(8,128)(2,1)S(1)} %all_to_all.26.po_ref), channel_id=1, source_target_pairs={{0,1},{1,0},{2,3},{3,2},{4,5},{5,4},{6,7},{7,6},{8,9},{9,8},{10,11... | collective-permute-start | bytes 6291464 | tf_op jit(solution)/shard_map/ppermute | solution.py:306
  77.9 3.9 %collective-permute-done.1.pt_ref = bf16[4,256,1024]{2,1,0:T(8,128)(2,1)} collective-permute-done((bf16[4,256,1024]{2,1,0:T(8,128)(2,1)S(1)}, bf16[4,256,1024]{2,1,0:T(8,128)(2,1)}, u32[]{:S(2)}, u32[]{:S(2)}) %collective-permute-start.1) | collective-permute-done | bytes 2097184 | tf_op jit(solution)/shard_map/ppermute | solution.py:306
  81.8 10.9 %all-gather.2.cloned.1.call-done.w_ref = bf16[8192,256]{1,0:T(8,128)(2,1)} async-done(((bf16[1024,256]{1,0:T(8,128)(2,1)}), bf16[8192,256]{1,0:T(8,128)(2,1)}) %all-gather.2.cloned.1.call-update) | async-done | bytes 4194320 | tf_op jit(solution)/shard_map/all_gather | solution.py:301
  92.7 5.7 %project_decode.1 = (bf16[2,128,128]{2,1,0:T(8,128)(2,1)}, bf16[2,128,128]{2,1,0:T(8,128)(2,1)}, bf16[8,80,128]{2,1,0:T(8,128)(2,1)S(1)}) custom-call(s32[3]{0:T(128)S(1)} %pad_add_fusion.at_ref, s32[2]{0:T(128)S(1)} %copy-done.5, s32[2,64]{1,0:T(2,128)S(1)} %copy-done.4, s32[2,64]{1,0:T(2,128)S(1)} %copy-done.6, ...), custom_call_target="tpu_custom_call" | custom-call | tf_op jit(solution)/shard_map/project_decode/pallas_call | solution.py:204
  98.4 14.4 %all_to_all.27.in_ref = bf16[8,80,128]{2,1,0:T(8,128)(2,1)S(1)} all-to-all(bf16[8,80,128]{2,1,0:T(8,128)(2,1)S(1)} %get-tuple-element.12), channel_id=1, replica_groups=mesh['z'=8,'y'=8,'x'=4,'c'=2] {'y'}, dimensions={0} | all-to-all | bytes 327680 | tf_op jit(solution)/shard_map/all_to_all | solution.py:322
  112.8 0.3 combine.1
  113.1 12.0 %all_to_all.28.in_ref = bf16[8,80,128]{2,1,0:T(8,128)(2,1)S(1)} all-to-all(bf16[8,80,128]{2,1,0:T(8,128)(2,1)S(1)} %combine.1), channel_id=1, replica_groups=mesh['z'=8,'y'=8,'x'=4,'c'=2] {'z'}, dimensions={0} | all-to-all | bytes 327680 | tf_op jit(solution)/shard_map/all_to_all | solution.py:323
  125.1 1.3 attend.1
  126.5 12.7 %all_to_all.29 = f32[8,8,128]{2,1,0:T(8,128)S(1)} all-to-all(f32[8,8,128]{2,1,0:T(8,128)S(1)} %attend.1), channel_id=1, replica_groups=mesh['z'=8,'y'=8,'x'=4,'c'=2] {'x','c'}, dimensions={0} | all-to-all | bytes 65536 | tf_op jit(solution)/shard_map/all_to_all | solution.py:324
  139.1 0.6 reduce_sum.9
  (7 shorter events, 0.0 us)
Async XLA Ops:
  7.2 28.3 %copy-start.1 = (bf16[2,1024,1,128]{3,1,2,0:T(8,128)(2,1)S(1)}, bf16[2,1024,1,128]{3,1,2,0:T(8,128)(2,1)}, u32[]{:S(2)}) copy-start(bf16[2,1024,1,128]{3,1,2,0:T(8,128)(2,1)} %param.13) | copy-start | bytes 1572868
  7.2 28.3 %copy-start = (bf16[2,1024,1,128]{3,1,2,0:T(8,128)(2,1)S(1)}, bf16[2,1024,1,128]{3,1,2,0:T(8,128)(2,1)}, u32[]{:S(2)}) copy-start(bf16[2,1024,1,128]{3,1,2,0:T(8,128)(2,1)} %param.12) | copy-start | bytes 1572868
  7.2 24.7 %copy-start.7 = (bf16[2,128,1,8,128]{4,3,2,1,0:T(8,128)(2,1)S(1)}, bf16[2,128,1,8,128]{4,3,2,1,0:T(8,128)(2,1)}, u32[]{:S(2)}) copy-start(bf16[2,128,1,8,128]{4,3,2,1,0:T(8,128)(2,1)} %param.17) | copy-start | bytes 1572868
  7.2 28.3 %copy-start.4 = (s32[2,64]{1,0:T(2,128)S(1)}, s32[2,64]{1,0:T(2,128)}, u32[]{:S(2)}) copy-start(s32[2,64]{1,0:T(2,128)} %ratio_ref.3) | copy-start | bytes 1540
  7.2 28.3 %copy-start.5 = (s32[2]{0:T(128)S(1)}, s32[2]{0:T(128)}, u32[]{:S(2)}) copy-start(s32[2]{0:T(128)} %phase_ref.3) | copy-start | bytes 28
  7.2 85.5 %all-gather.2.cloned.1.call-start = ((), (), s32[]{:S(2)}) async-start(), calls=%async_computation.5 | async-start | bytes 4718592 | tf_op jit(solution)/shard_map/all_gather | solution.py:301
  30.5 5.1 %collective-permute-start = (bf16[2,2,256,128]{3,2,1,0:T(8,128)(2,1)}, bf16[2,2,256,128]{3,2,1,0:T(8,128)(2,1)S(1)}, u32[]{:S(2)}, u32[]{:S(2)}) collective-permute-start(bf16[2,2,256,128]{3,2,1,0:T(8,128)(2,1)} %get-tuple-element.8), channel_id=1, source_target_pairs={{0,8},{8,16},{16,24},{24,32},{32,40},{40,48},{48,56},{56,64},{64,7... | collective-permute-start | bytes 786440 | tf_op jit(solution)/shard_map/ppermute | solution.py:299
  41.9 36.0 %copy-start.8 = (bf16[4,2,1,8,128]{4,3,2,1,0:T(8,128)(2,1)S(1)}, bf16[4,2,1,8,128]{4,3,2,1,0:T(8,128)(2,1)}, u32[]{:S(2)}) copy-start(bf16[4,2,1,8,128]{4,3,2,1,0:T(8,128)(2,1)} %param.22) | copy-start | bytes 49156
  41.9 50.8 %copy-start.2 = (bf16[2,256,1,128]{3,1,2,0:T(8,128)(2,1)S(1)}, bf16[2,256,1,128]{3,1,2,0:T(8,128)(2,1)}, u32[]{:S(2)}) copy-start(bf16[2,256,1,128]{3,1,2,0:T(8,128)(2,1)} %param.20) | copy-start | bytes 393220
  41.9 50.8 %copy-start.3 = (bf16[2,256,1,128]{3,1,2,0:T(8,128)(2,1)S(1)}, bf16[2,256,1,128]{3,1,2,0:T(8,128)(2,1)}, u32[]{:S(2)}) copy-start(bf16[2,256,1,128]{3,1,2,0:T(8,128)(2,1)} %param.21) | copy-start | bytes 393220
  41.9 50.8 %copy-start.6 = (s32[2,64]{1,0:T(2,128)S(1)}, s32[2,64]{1,0:T(2,128)}, u32[]{:S(2)}) copy-start(s32[2,64]{1,0:T(2,128)} %len_ref.1) | copy-start | bytes 1540
  70.7 11.1 %collective-permute-start.1 = (bf16[4,256,1024]{2,1,0:T(8,128)(2,1)S(1)}, bf16[4,256,1024]{2,1,0:T(8,128)(2,1)}, u32[]{:S(2)}, u32[]{:S(2)}) collective-permute-start(bf16[4,256,1024]{2,1,0:T(8,128)(2,1)S(1)} %all_to_all.26.po_ref), channel_id=1, source_target_pairs={{0,1},{1,0},{2,3},{3,2},{4,5},{5,4},{6,7},{7,6},{8,9},{9,8},{10,11... | collective-permute-start | bytes 6291464 | tf_op jit(solution)/shard_map/ppermute | solution.py:306
Sparse Core Ops, SparseCore 0:
  30.6 62.0 all-gather.1

commit v3 on v2

--- a/solution.py
+++ b/solution.py
@@ -31,31 +31,33 @@
     return jnp.dot(a, b, preferred_element_type=F32)
 
 
-def stage_kernel(wk_ref, wv_ref, tk_ref, tv_ref, w_ref, tails_ref):
+def stage_kernel(wk_ref, wv_ref, out_ref):
     for copy in range(8):
-        w_ref[copy, :, :HD] = wk_ref[...]
-        w_ref[copy, :, HD:] = wv_ref[...]
-    tails_ref[0] = tk_ref[...]
-    tails_ref[1] = tv_ref[...]
-
-
-def stage(wk, wv, raw_k, raw_v):
-    tail = pl.BlockSpec((REQ, OFF, HD), lambda i: (0, INTERVAL // OFF - 1, 0))
-    weight = pl.BlockSpec((HD, HD), lambda i: (0, 0))
-    return pl.pallas_call(
-        stage_kernel,
-        out_shape=(
-            jax.ShapeDtypeStruct((8, HD, 2 * HD), BF),
-            jax.ShapeDtypeStruct((2, REQ, OFF, HD), BF),
-        ),
+        out_ref[copy, :, :HD] = wk_ref[...]
+        out_ref[copy, :, HD:] = wv_ref[...]
+
+
+def stage(wk, wv):
+    return pl.pallas_call(
+        stage_kernel, out_shape=pltpu.VMEM((8, HD, 2 * HD), BF), name="stage"
+    )(wk, wv)
+
+
+def tail_kernel(tk_ref, tv_ref, out_ref):
+    out_ref[0] = tk_ref[...]
+    out_ref[1] = tv_ref[...]
+
+
+def tail(raw_k, raw_v):
+    window = pl.BlockSpec((REQ, OFF, HD), lambda i: (0, INTERVAL // OFF - 1, 0))
+    return pl.pallas_call(
+        tail_kernel,
+        out_shape=pltpu.VMEM((2, REQ, OFF, HD), BF),
         grid=(1,),
-        in_specs=[weight, weight, tail, tail],
-        out_specs=(
-            pl.BlockSpec((8, HD, 2 * HD), lambda i: (0, 0, 0)),
-            pl.BlockSpec((2, REQ, OFF, HD), lambda i: (0, 0, 0, 0)),
-        ),
-        name="stage",
-    )(wk, wv, raw_k, raw_v)
+        in_specs=[window, window],
+        out_specs=pl.BlockSpec((2, REQ, OFF, HD), lambda i: (0, 0, 0, 0)),
+        name="tail",
+    )(raw_k, raw_v)
 
 
 def pool_kernel(at_ref, phase_ref, ratio_ref, q_ref, rk_ref, rv_ref, near_ref, out_ref):
@@ -138,7 +140,7 @@
 
 def decode_kernel(
     at_ref, phase_ref, ratio_ref, len_ref,
-    po_ref, pt_ref, w_ref, q_ref, sk_ref, sv_ref, rk_ref, rv_ref,
+    po_ref, pt_ref, w_ref, q_ref, sk_ref, sv_ref, tails_ref,
     bk_ref, bv_ref, out_ref, held, other, sems, other_sems,
 ):
     shard, core, last = at_ref[0], at_ref[1], at_ref[2]
@@ -167,7 +169,7 @@
         mine = of_row == r
         leftover = jnp.where(last == 1, OFF - phase_ref[r], OFF)
         early.append(score(sk_ref[r], mine & (col < len_ref[r, shard])))
-        early.append(score(rk_ref[r], mine & (col >= leftover)))
+        early.append(score(tails_ref[0, r], mine & (col >= leftover)))
     total_part = 0.0
     for x in range(4):
         copies[2 * x].wait()
@@ -187,7 +189,7 @@
     weights = jnp.exp2(scores - peak)
     total = jnp.sum(weights, axis=1, keepdims=True)
     weights = weights.astype(BF)
-    values = [sv_ref[0], rv_ref[0], sv_ref[1], rv_ref[1], made[0][:, HD:], made[1][:, HD:]]
+    values = [sv_ref[0], tails_ref[1, 0], sv_ref[1], tails_ref[1, 1], made[0][:, HD:], made[1][:, HD:]]
     weighted, at = 0.0, 0
     for v in values:
         weighted += dot_nn(weights[:, at : at + v.shape[0]], v)
@@ -198,41 +200,26 @@
     pack(out_ref, weighted, rows[0:1], rows[1:2])
 
 
-def project_decode(at, phase, ratio, length, p_own, p_other, weights, queries, res_k, res_v, raw_k, raw_v):
-    whole = lambda i, *_: (0, 0, 0)
-    tail = pl.BlockSpec((REQ, OFF, HD), lambda i, *_: (0, INTERVAL // OFF - 1, 0))
+def project_decode(at, phase, ratio, length, p_own, p_other, weights, queries, res_k, res_v, tails):
+    here = lambda array: pltpu.with_memory_space_constraint(array, pltpu.VMEM)
+    far = lambda array: pltpu.with_memory_space_constraint(array, pltpu.HBM)
+    scalar, vmem = pl.BlockSpec(memory_space=pltpu.SMEM), pl.BlockSpec(memory_space=pltpu.VMEM)
+    hbm = pl.BlockSpec(memory_space=pltpu.HBM)
     return pl.pallas_call(
         decode_kernel,
         out_shape=(
-            jax.ShapeDtypeStruct((REQ, NB, HD), BF),
-            jax.ShapeDtypeStruct((REQ, NB, HD), BF),
-            jax.ShapeDtypeStruct((8, ROWS + 16, HD), BF),
+            pltpu.VMEM((REQ, NB, HD), BF),
+            pltpu.VMEM((REQ, NB, HD), BF),
+            pltpu.VMEM((8, ROWS + 16, HD), BF),
         ),
-        grid_spec=pltpu.PrefetchScalarGridSpec(
-            num_scalar_prefetch=4,
-            grid=(1,),
-            in_specs=[
-                pl.BlockSpec((4, REQ * NB, G * HD), whole),
-                pl.BlockSpec(memory_space=pltpu.HBM),
-                pl.BlockSpec(memory_space=pltpu.HBM),
-                pl.BlockSpec((ROWS, HD), lambda i, *_: (0, 0)),
-                pl.BlockSpec((REQ, RES, HD), whole),
-                pl.BlockSpec((REQ, RES, HD), whole),
-                tail,
-                tail,
-            ],
-            out_specs=[
-                pl.BlockSpec((REQ, NB, HD), whole),
-                pl.BlockSpec((REQ, NB, HD), whole),
-                pl.BlockSpec((8, ROWS + 16, HD), whole),
-            ],
-            scratch_shapes=[
-                pltpu.VMEM((8, G * HD, 2 * HD), BF),
-                pltpu.VMEM((4, REQ * NB, G * HD), BF),
-                pltpu.SemaphoreType.DMA((8,)),
-                pltpu.SemaphoreType.DMA((4,)),
-            ],
-        ),
+        in_specs=[scalar] * 4 + [vmem, hbm, hbm] + [vmem] * 4,
+        out_specs=(vmem, vmem, vmem),
+        scratch_shapes=[
+            pltpu.VMEM((8, G * HD, 2 * HD), BF),
+            pltpu.VMEM((4, REQ * NB, G * HD), BF),
+            pltpu.SemaphoreType.DMA((8,)),
+            pltpu.SemaphoreType.DMA((4,)),
+        ],
         compiler_params=pltpu.CompilerParams(vmem_limit_bytes=40 << 20),
         name="project_decode",
     )(
@@ -240,14 +227,13 @@
         phase,
         ratio,
         length,
-        p_own,
-        pltpu.with_memory_space_constraint(p_other, pltpu.HBM),
-        pltpu.with_memory_space_constraint(weights, pltpu.HBM),
-        queries,
-        res_k,
-        res_v,
-        raw_k,
-        raw_v,
+        here(p_own),
+        far(p_other),
+        far(weights),
+        here(queries),
+        here(res_k),
+        here(res_v),
+        here(tails),
     )
 
 
@@ -266,16 +252,33 @@
     rows = STEPS * REQ
     flat = jnp.concatenate([attended[g * rows : (g + 1) * rows] for g in range(G)], axis=1)
     part = dot_nn(flat.astype(BF), w_ref[...])
+    high = part.astype(BF)
+    both = jnp.concatenate([high.astype(F32), part - high.astype(F32)], axis=0).astype(BF)
     for copy in range(8):
-        out_ref[copy] = part
+        out_ref[copy] = both
 
 
 def attend(state, out_weight):
     return pl.pallas_call(
         attend_kernel,
-        out_shape=pltpu.VMEM((8, STEPS * REQ, HD), F32),
+        out_shape=pltpu.VMEM((8, 2 * STEPS * REQ, HD), BF),
         name="attend",
-    )(pltpu.with_memory_space_constraint(state, pltpu.VMEM), out_weight)
+    )(
+        pltpu.with_memory_space_constraint(state, pltpu.VMEM),
+        pltpu.with_memory_space_constraint(out_weight, pltpu.VMEM),
+    )
+
+
+def total_kernel(in_ref, out_ref):
+    rows = STEPS * REQ
+    both = jnp.sum(in_ref[...].astype(F32), axis=0)
+    out_ref[...] = (both[:rows] + both[rows:]).astype(BF)
+
+
+def total(parts):
+    return pl.pallas_call(
+        total_kernel, out_shape=jax.ShapeDtypeStruct((STEPS * REQ, HD), BF), name="total"
+    )(pltpu.with_memory_space_constraint(parts, pltpu.VMEM))
 
 
 def body(
@@ -295,7 +298,8 @@
     shard = lax.axis_index(SEQ)
     count = lax.axis_size(SEQ)
     raw_k, raw_v = raw_keys[:, :, 0], raw_values[:, :, 0]
-    staged, tails = stage(beacon_wk, beacon_wv, raw_k, raw_v)
+    staged = stage(beacon_wk, beacon_wv)
+    tails = tail(raw_k, raw_v)
     near = lax.ppermute(tails, SEQ, [(i, i + 1) for i in range(count - 1)])
     column = lax.all_to_all(staged, "y", 0, 0).reshape(8 * HD, 2 * HD)
     weights = lax.all_gather(column, "z", axis=0, tiled=True)
@@ -316,13 +320,12 @@
         step_queries,
         resident_keys[:, :, 0],
         resident_values[:, :, 0],
-        raw_k,
-        raw_v,
+        tails,
     )
     state = combine(lax.all_to_all(state, "y", 0, 0))
     parts = attend(lax.all_to_all(state, "z", 0, 0), out_weight)
     parts = lax.all_to_all(parts, ("x", "c"), 0, 0)
-    projected = jnp.sum(parts, axis=0).astype(BF).reshape(STEPS, REQ, HD)
+    projected = total(parts).reshape(STEPS, REQ, HD)
     return beacon_k[:, :, None], beacon_v[:, :, None], projected
 
 

time: 147 us -> 145 us (0.986)
  blocking collectives: 88.9 us -> 76.1 us
  starting transfers between devices: 8.73 us -> 16.9 us
  waiting for transfers between devices: 18.2 us -> 20.6 us
    all_to_all x1 -> x0, blocking collectives: 12.7 us -> none  [body(): parts = lax.all_to_all(parts, ('x', 'c'), 0, 0)]
    all_to_all x0 -> x1, starting transfers between devices: none -> 8.15 us  [body(): parts = lax.all_to_all(parts, ('x', 'c'), 0, 0)]
    all_to_all x0 -> x1, waiting for transfers between devices: none -> 3.46 us  [body(): parts = lax.all_to_all(parts, ('x', 'c'), 0, 0)]
    pallas_call x3 -> x5, Pallas kernels: 9.12 us -> 8.73 us  [the longest x1 5.24 us: project_decode(): pl.pallas_call(decode_kernel, out_shape=(pltpu.VMEM((REQ, NB, HD), BF), p...]
  transfers between devices with their start and end apart: 3 -> 4, of which waited for: 3 -> 4; matrix products, arithmetic and copies ran while one was open for 0% -> 1% of each run, Pallas kernels for 4% -> 5%
where the time goes in v3:
time: 145 us
  blocking collectives  76.1 us (52%)
  waiting for transfers between devices  20.6 us (14%)
  starting transfers between devices  16.9 us (12%)
  Pallas kernels  15.4 us (11%)
  between operations  14.2 us (10%)
    all_to_all x1, blocking collectives, body(): p_own = lax.all_to_all(pooled, 'x', 0, 0)  27.6 us
    all_to_all x1, blocking collectives, body(): column = lax.all_to_all(staged, 'y', 0, 0).reshape(8 * HD, 2 * HD)  22.1 us
    all_to_all x1, blocking collectives, body(): state = combine(lax.all_to_all(state, 'y', 0, 0))  14.4 us
    all_to_all x1, blocking collectives, body(): parts = attend(lax.all_to_all(state, 'z', 0, 0), out_weight)  12 us
    all_gather x1, waiting for transfers between devices, body(): weights = lax.all_gather(column, 'z', axis=0, tiled=True)  10.2 us
    all_to_all x1, starting transfers between devices, body(): parts = lax.all_to_all(parts, ('x', 'c'), 0, 0)  8.15 us
    ppermute x1, starting transfers between devices, body(): p_other = lax.ppermute(p_own, 'c', [(0, 1), (1, 0)])  7.24 us
    pallas_call x1, Pallas kernels, pool(): pl.pallas_call(pool_kernel, out_shape=jax.ShapeDtypeStruct((4, REQ * NB,...  6.37 us
  transfers between devices with their start and end apart: 4, of which 4 were waited for; matrix products, arithmetic and copies ran while one was open for 1% of the time, Pallas kernels for 5%

profile of v3, /device:TPU:1, one launch (start us, length us, event | category | flops | bytes accessed | tf_op | source)
XLA Modules:
  0.0 144.8 jit_solution(12499656964653848818)
XLA Ops:
  7.2 0.0 all-gather.2.cloned.1.call-start
  7.2 0.9 stage.1
  8.1 0.0 copy-start
  8.1 0.0 copy-start.1
  8.1 0.0 copy-start.5
  8.2 0.0 copy-start.6
  8.2 22.1 %all_to_all.25 = bf16[8,128,256]{2,1,0:T(8,128)(2,1)} all-to-all(bf16[8,128,256]{2,1,0:T(8,128)(2,1)S(1)} %stage.1), channel_id=1, replica_groups=mesh['z'=8,'y'=8,'x'=4,'c'=2] {'y'}, dimensions={0} | all-to-all | bytes 1048576 | tf_op jit(solution)/shard_map/all_to_all | solution.py:304
  30.3 0.0 all-gather.2.cloned.1.call-update
  30.3 1.0 tail.1.tails_ref
  31.3 1.5 %collective-permute-start = (bf16[2,2,256,128]{3,2,1,0:T(8,128)(2,1)S(1)}, bf16[2,2,256,128]{3,2,1,0:T(8,128)(2,1)S(1)}, u32[]{:S(2)}, u32[]{:S(2)}) collective-permute-start(bf16[2,2,256,128]{3,2,1,0:T(8,128)(2,1)S(1)} %tail.1.tails_ref), channel_id=1, source_target_pairs={{0,8},{8,16},{16,24},{24,32},{32,40},{40,48},{48,56},{56,64},{64,7... | collective-permute-start | bytes 786440 | tf_op jit(solution)/shard_map/ppermute | solution.py:303
  32.8 0.1 copy.20
  32.9 0.1 pad_add_fusion.at_ref
  33.0 3.1 %collective-permute-done.near_ref = bf16[2,2,256,128]{3,2,1,0:T(8,128)(2,1)S(1)} collective-permute-done((bf16[2,2,256,128]{3,2,1,0:T(8,128)(2,1)S(1)}, bf16[2,2,256,128]{3,2,1,0:T(8,128)(2,1)S(1)}, u32[]{:S(2)}, u32[]{:S(2)}) %collective-permute-start) | collective-permute-done | bytes 262176 | tf_op jit(solution)/shard_map/ppermute | solution.py:303
  36.1 6.4 %pool.1 = bf16[4,256,1024]{2,1,0:T(8,128)(2,1)S(1)} custom-call(s32[3]{0:T(128)S(1)} %pad_add_fusion.at_ref, s32[2]{0:T(128)S(1)} %copy-done.6, s32[2,64]{1,0:T(2,128)S(1)} %copy-done.5, bf16[2,8,128,128]{3,2,1,0:T(8,128)(2,1)S(1)} %bitcast.30, bf16[2,1024,128]{2,1,0:T(8,128)(2,1)S(1)} %bitcast.27, bf16[2,1024,128]{2,1,0:T(8,128)(2,1)S(1)} %bitcast.29, ...), custom_call_target="tpu_custom_call" | custom-call | tf_op jit(solution)/shard_map/pool/pallas_call | solution.py:90
  42.5 0.0 copy-start.9
  42.5 0.0 copy-start.3
  42.5 0.0 copy-start.4
  42.5 0.0 copy-start.7
  42.5 27.6 %all_to_all.26.po_ref = bf16[4,256,1024]{2,1,0:T(8,128)(2,1)S(1)} all-to-all(bf16[4,256,1024]{2,1,0:T(8,128)(2,1)S(1)} %pool.1), channel_id=1, replica_groups=mesh['z'=8,'y'=8,'x'=4,'c'=2] {'x'}, dimensions={0} | all-to-all | bytes 4194304 | tf_op jit(solution)/shard_map/all_to_all | solution.py:309
  70.1 7.2 %collective-permute-start.1 = (bf16[4,256,1024]{2,1,0:T(8,128)(2,1)S(1)}, bf16[4,256,1024]{2,1,0:T(8,128)(2,1)}, u32[]{:S(2)}, u32[]{:S(2)}) collective-permute-start(bf16[4,256,1024]{2,1,0:T(8,128)(2,1)S(1)} %all_to_all.26.po_ref), channel_id=1, source_target_pairs={{0,1},{1,0},{2,3},{3,2},{4,5},{5,4},{6,7},{7,6},{8,9},{9,8},{10,11... | collective-permute-start | bytes 6291464 | tf_op jit(solution)/shard_map/ppermute | solution.py:310
  77.4 3.9 %collective-permute-done.1.pt_ref = bf16[4,256,1024]{2,1,0:T(8,128)(2,1)} collective-permute-done((bf16[4,256,1024]{2,1,0:T(8,128)(2,1)S(1)}, bf16[4,256,1024]{2,1,0:T(8,128)(2,1)}, u32[]{:S(2)}, u32[]{:S(2)}) %collective-permute-start.1) | collective-permute-done | bytes 2097184 | tf_op jit(solution)/shard_map/ppermute | solution.py:310
  81.3 10.2 %all-gather.2.cloned.1.call-done.w_ref = bf16[8192,256]{1,0:T(8,128)(2,1)} async-done(((bf16[1024,256]{1,0:T(8,128)(2,1)}), bf16[8192,256]{1,0:T(8,128)(2,1)}) %all-gather.2.cloned.1.call-update) | async-done | bytes 4194320 | tf_op jit(solution)/shard_map/all_gather | solution.py:305
  91.5 5.2 %project_decode.1 = (bf16[2,128,128]{2,1,0:T(8,128)(2,1)S(1)}, bf16[2,128,128]{2,1,0:T(8,128)(2,1)S(1)}, bf16[8,80,128]{2,1,0:T(8,128)(2,1)S(1)}) custom-call(s32[3]{0:T(128)S(1)} %pad_add_fusion.at_ref, s32[2]{0:T(128)S(1)} %copy-done.6, s32[2,64]{1,0:T(2,128)S(1)} %copy-done.5, s32[2,64]{1,0:T(2,128)S(1)} %copy-done.7, ...), custom_call_target="tpu_custom_call" | custom-call | tf_op jit(solution)/shard_map/project_decode/pallas_call | solution.py:208
  96.7 14.4 %all_to_all.27.in_ref = bf16[8,80,128]{2,1,0:T(8,128)(2,1)S(1)} all-to-all(bf16[8,80,128]{2,1,0:T(8,128)(2,1)S(1)} %get-tuple-element.8), channel_id=1, replica_groups=mesh['z'=8,'y'=8,'x'=4,'c'=2] {'y'}, dimensions={0} | all-to-all | bytes 327680 | tf_op jit(solution)/shard_map/all_to_all | solution.py:325
  111.1 0.3 combine.1
  111.4 12.0 %all_to_all.28.in_ref = bf16[8,80,128]{2,1,0:T(8,128)(2,1)S(1)} all-to-all(bf16[8,80,128]{2,1,0:T(8,128)(2,1)S(1)} %combine.1), channel_id=1, replica_groups=mesh['z'=8,'y'=8,'x'=4,'c'=2] {'z'}, dimensions={0} | all-to-all | bytes 327680 | tf_op jit(solution)/shard_map/all_to_all | solution.py:326
  123.4 1.0 attend.1
  124.5 8.1 %all-to-all-start.4 = ((bf16[8,16,128]{2,1,0:T(8,128)(2,1)}), bf16[8,16,128]{2,1,0:T(8,128)(2,1)S(1)}, u32[]{:S(2)}, u32[]{:S(2)}) async-start(bf16[8,16,128]{2,1,0:T(8,128)(2,1)} %attend.1), calls=%async_computation.4 | async-start | bytes 65536 | tf_op jit(solution)/shard_map/all_to_all | solution.py:327
  132.6 0.6 copy.21
  133.2 0.6 copy.22
  133.9 3.5 %all-to-all-done.4.in_ref = bf16[8,16,128]{2,1,0:T(8,128)(2,1)S(1)} async-done(((bf16[8,16,128]{2,1,0:T(8,128)(2,1)}), bf16[8,16,128]{2,1,0:T(8,128)(2,1)S(1)}, u32[]{:S(2)}, u32[]{:S(2)}) %all-to-all-start.4) | async-done | bytes 32800 | tf_op jit(solution)/shard_map/all_to_all | solution.py:327
  137.3 0.6 total.1
  (13 shorter events, 0.0 us)
Async XLA Ops:
  7.2 25.7 %copy-start.8 = (bf16[2,128,1,8,128]{4,3,2,1,0:T(8,128)(2,1)S(1)}, bf16[2,128,1,8,128]{4,3,2,1,0:T(8,128)(2,1)}, u32[]{:S(2)}) copy-start(bf16[2,128,1,8,128]{4,3,2,1,0:T(8,128)(2,1)} %param.17) | copy-start | bytes 1572868
  7.2 84.3 %all-gather.2.cloned.1.call-start = ((), (), s32[]{:S(2)}) async-start(), calls=%async_computation.5 | async-start | bytes 4718592 | tf_op jit(solution)/shard_map/all_gather | solution.py:305
  8.1 28.0 %copy-start = (bf16[2,1024,1,128]{3,1,2,0:T(8,128)(2,1)S(1)}, bf16[2,1024,1,128]{3,1,2,0:T(8,128)(2,1)}, u32[]{:S(2)}) copy-start(bf16[2,1024,1,128]{3,1,2,0:T(8,128)(2,1)} %param.12) | copy-start | bytes 1572868
  8.1 28.0 %copy-start.1 = (bf16[2,1024,1,128]{3,1,2,0:T(8,128)(2,1)S(1)}, bf16[2,1024,1,128]{3,1,2,0:T(8,128)(2,1)}, u32[]{:S(2)}) copy-start(bf16[2,1024,1,128]{3,1,2,0:T(8,128)(2,1)} %param.13) | copy-start | bytes 1572868
  8.1 28.0 %copy-start.5 = (s32[2,64]{1,0:T(2,128)S(1)}, s32[2,64]{1,0:T(2,128)}, u32[]{:S(2)}) copy-start(s32[2,64]{1,0:T(2,128)} %ratio_ref.3) | copy-start | bytes 1540
  8.2 28.0 %copy-start.6 = (s32[2]{0:T(128)S(1)}, s32[2]{0:T(128)}, u32[]{:S(2)}) copy-start(s32[2]{0:T(128)} %phase_ref.3) | copy-start | bytes 28
  31.3 4.8 %collective-permute-start = (bf16[2,2,256,128]{3,2,1,0:T(8,128)(2,1)S(1)}, bf16[2,2,256,128]{3,2,1,0:T(8,128)(2,1)S(1)}, u32[]{:S(2)}, u32[]{:S(2)}) collective-permute-start(bf16[2,2,256,128]{3,2,1,0:T(8,128)(2,1)S(1)} %tail.1.tails_ref), channel_id=1, source_target_pairs={{0,8},{8,16},{16,24},{24,32},{32,40},{40,48},{48,56},{56,64},{64,7... | collective-permute-start | bytes 786440 | tf_op jit(solution)/shard_map/ppermute | solution.py:303
  42.5 34.9 %copy-start.9 = (bf16[4,2,1,8,128]{4,3,2,1,0:T(8,128)(2,1)S(1)}, bf16[4,2,1,8,128]{4,3,2,1,0:T(8,128)(2,1)}, u32[]{:S(2)}) copy-start(bf16[4,2,1,8,128]{4,3,2,1,0:T(8,128)(2,1)} %param.22) | copy-start | bytes 49156
  42.5 49.0 %copy-start.3 = (bf16[2,256,1,128]{3,1,2,0:T(8,128)(2,1)S(1)}, bf16[2,256,1,128]{3,1,2,0:T(8,128)(2,1)}, u32[]{:S(2)}) copy-start(bf16[2,256,1,128]{3,1,2,0:T(8,128)(2,1)} %param.20) | copy-start | bytes 393220
  42.5 48.9 %copy-start.4 = (bf16[2,256,1,128]{3,1,2,0:T(8,128)(2,1)S(1)}, bf16[2,256,1,128]{3,1,2,0:T(8,128)(2,1)}, u32[]{:S(2)}) copy-start(bf16[2,256,1,128]{3,1,2,0:T(8,128)(2,1)} %param.21) | copy-start | bytes 393220
  42.5 48.9 %copy-start.7 = (s32[2,64]{1,0:T(2,128)S(1)}, s32[2,64]{1,0:T(2,128)}, u32[]{:S(2)}) copy-start(s32[2,64]{1,0:T(2,128)} %len_ref.1) | copy-start | bytes 1540
  70.1 11.1 %collective-permute-start.1 = (bf16[4,256,1024]{2,1,0:T(8,128)(2,1)S(1)}, bf16[4,256,1024]{2,1,0:T(8,128)(2,1)}, u32[]{:S(2)}, u32[]{:S(2)}) collective-permute-start(bf16[4,256,1024]{2,1,0:T(8,128)(2,1)S(1)} %all_to_all.26.po_ref), channel_id=1, source_target_pairs={{0,1},{1,0},{2,3},{3,2},{4,5},{5,4},{6,7},{7,6},{8,9},{9,8},{10,11... | collective-permute-start | bytes 6291464 | tf_op jit(solution)/shard_map/ppermute | solution.py:310
  91.5 32.0 %copy-start.2 = (bf16[1024,128]{1,0:T(8,128)(2,1)S(1)}, bf16[1024,128]{1,0:T(8,128)(2,1)}, u32[]{:S(2)}) copy-start(bf16[1024,128]{1,0:T(8,128)(2,1)} %w_ref.1) | copy-start | bytes 786436
  124.5 12.9 %all-to-all-start.4 = ((bf16[8,16,128]{2,1,0:T(8,128)(2,1)}), bf16[8,16,128]{2,1,0:T(8,128)(2,1)S(1)}, u32[]{:S(2)}, u32[]{:S(2)}) async-start(bf16[8,16,128]{2,1,0:T(8,128)(2,1)} %attend.1), calls=%async_computation.4 | async-start | bytes 65536 | tf_op jit(solution)/shard_map/all_to_all | solution.py:327
Sparse Core Ops, SparseCore 0:
  30.4 60.9 all-gather.1

commit v4 on v3

--- a/solution.py
+++ b/solution.py
@@ -19,6 +19,7 @@
 SCALE = math.log2(math.e) / math.sqrt(HD)
 MASKED = -1e30
 SEQ = ("z", "y")
+ALL = ("z", "y", "x", "c")
 BF = jnp.bfloat16
 F32 = jnp.float32
 
@@ -60,25 +61,47 @@
     )(raw_k, raw_v)
 
 
-def pool_kernel(at_ref, phase_ref, ratio_ref, q_ref, rk_ref, rv_ref, near_ref, out_ref):
+def pool_bounds(at_ref, phase_ref, ratio_ref, start_col, width):
     r = pl.program_id(0)
-    shard = at_ref[0]
-    phase, step = phase_ref[r], ratio_ref[r, shard]
+    phase, step = phase_ref[r], ratio_ref[r, at_ref[0]]
     start = OFF - phase
-    low = start + jnp.where(shard == 0, phase, 0)
-    col = lax.broadcasted_iota(jnp.int32, (2 * NB, OFF + INTERVAL), 1)
-    slot = lax.broadcasted_iota(jnp.int32, (2 * NB, OFF + INTERVAL), 0) % NB
+    low = start + jnp.where(at_ref[0] == 0, phase, 0)
+    col = lax.broadcasted_iota(jnp.int32, (2 * NB, width), 1) + start_col
+    slot = lax.broadcasted_iota(jnp.int32, (2 * NB, width), 0) % NB
     bound = jnp.minimum(low + (slot + 1) * step, start + INTERVAL)
-    allowed = (col >= low) & (col < bound)
+    return (col >= low) & (col < bound)
+
+
+def pool_rows(q, keys, allowed):
+    scores = jnp.where(allowed, dot_nt(q, keys) * SCALE, MASKED)
+    return scores, jnp.max(scores, axis=1, keepdims=True)
+
+
+def own_kernel(at_ref, phase_ref, ratio_ref, q_ref, rk_ref, rv_ref, sum_ref, stat_ref):
+    allowed = pool_bounds(at_ref, phase_ref, ratio_ref, OFF, INTERVAL)
+    lane = lax.broadcasted_iota(jnp.int32, (2 * NB, HD), 1)
     for pair in range(G // 2):
         q = q_ref[0, 2 * pair : 2 * pair + 2].reshape(2 * NB, HD)
-        scores = jnp.concatenate([dot_nt(q, near_ref[0, 0]), dot_nt(q, rk_ref[0])], axis=1)
-        scores = jnp.where(allowed, scores * SCALE, MASKED)
-        peak = jnp.max(scores, axis=1, keepdims=True)
+        scores, peak = pool_rows(q, rk_ref[0], allowed)
         weights = jnp.exp2(scores - peak)
         total = jnp.sum(weights, axis=1, keepdims=True)
-        weights = weights.astype(BF)
-        weighted = dot_nn(weights[:, :OFF], near_ref[1, 0]) + dot_nn(weights[:, OFF:], rv_ref[0])
+        rows = slice(2 * pair * NB, (2 * pair + 2) * NB)
+        sum_ref[0, rows] = dot_nn(weights.astype(BF), rv_ref[0])
+        stat_ref[0, rows] = jnp.where(lane == 0, peak, total)
+
+
+def rest_kernel(at_ref, phase_ref, ratio_ref, q_ref, near_ref, sum_ref, stat_ref, out_ref):
+    allowed = pool_bounds(at_ref, phase_ref, ratio_ref, 0, OFF)
+    for pair in range(G // 2):
+        q = q_ref[0, 2 * pair : 2 * pair + 2].reshape(2 * NB, HD)
+        scores, near_peak = pool_rows(q, near_ref[0, 0], allowed)
+        rows = slice(2 * pair * NB, (2 * pair + 2) * NB)
+        own_peak, own_total = stat_ref[0, rows, 0:1], stat_ref[0, rows, 1:2]
+        peak = jnp.maximum(near_peak, own_peak)
+        weights = jnp.exp2(scores - peak)
+        factor = jnp.exp2(own_peak - peak)
+        total = jnp.sum(weights, axis=1, keepdims=True) + own_total * factor
+        weighted = dot_nn(weights.astype(BF), near_ref[1, 0]) + sum_ref[0, rows] * factor
         pooled = (weighted / total).astype(BF)
         for copy in range(4):
             for half in range(2):
@@ -86,24 +109,44 @@
                 out_ref[copy, :, at : at + HD] = pooled[half * NB : (half + 1) * NB]
 
 
-def pool(at, phase, ratio, queries, raw_k, raw_v, near):
-    return pl.pallas_call(
-        pool_kernel,
+QUERIES = pl.BlockSpec((1, G, NB, HD), lambda r, *_: (r, 0, 0, 0))
+STATE = pl.BlockSpec((1, G * NB, HD), lambda r, *_: (r, 0, 0))
+
+
+def pool_own(at, phase, ratio, queries, raw_k, raw_v):
+    rows = pl.BlockSpec((1, INTERVAL, HD), lambda r, *_: (r, 0, 0))
+    return pl.pallas_call(
+        own_kernel,
+        out_shape=(jax.ShapeDtypeStruct((REQ, G * NB, HD), F32),) * 2,
+        grid_spec=pltpu.PrefetchScalarGridSpec(
+            num_scalar_prefetch=3,
+            grid=(REQ,),
+            in_specs=[QUERIES, rows, rows],
+            out_specs=(STATE, STATE),
+        ),
+        compiler_params=pltpu.CompilerParams(vmem_limit_bytes=24 << 20),
+        name="pool_own",
+    )(at, phase, ratio, queries, raw_k, raw_v)
+
+
+def pool_rest(at, phase, ratio, queries, near, sums, stats):
+    return pl.pallas_call(
+        rest_kernel,
         out_shape=jax.ShapeDtypeStruct((4, REQ * NB, G * HD), BF),
         grid_spec=pltpu.PrefetchScalarGridSpec(
             num_scalar_prefetch=3,
             grid=(REQ,),
             in_specs=[
-                pl.BlockSpec((1, G, NB, HD), lambda r, *_: (r, 0, 0, 0)),
-                pl.BlockSpec((1, INTERVAL, HD), lambda r, *_: (r, 0, 0)),
-                pl.BlockSpec((1, INTERVAL, HD), lambda r, *_: (r, 0, 0)),
+                QUERIES,
                 pl.BlockSpec((2, 1, OFF, HD), lambda r, *_: (0, r, 0, 0)),
+                STATE,
+                STATE,
             ],
             out_specs=pl.BlockSpec((4, NB, G * HD), lambda r, *_: (0, r, 0)),
         ),
-        compiler_params=pltpu.CompilerParams(vmem_limit_bytes=40 << 20),
-        name="pool",
-    )(at, phase, ratio, queries, raw_k, raw_v, near)
+        compiler_params=pltpu.CompilerParams(vmem_limit_bytes=24 << 20),
+        name="pool_rest",
+    )(at, phase, ratio, queries, near, sums, stats)
 
 
 def pieces(value):
@@ -144,17 +187,24 @@
     bk_ref, bv_ref, out_ref, held, other, sems, other_sems,
 ):
     shard, core, last = at_ref[0], at_ref[1], at_ref[2]
-    copies = [
-        pltpu.make_async_copy(w_ref.at[pl.ds(k * G * HD, G * HD)], held.at[k], sems.at[k])
-        for k in range(8)
-    ]
+    copies = [pltpu.make_async_copy(w_ref.at[k], held.at[k], sems.at[k]) for k in range(8)]
+    turned = [pltpu.make_async_copy(w_ref.at[:, k], held.at[k], sems.at[k]) for k in range(8)]
     other_copies = [
         pltpu.make_async_copy(pt_ref.at[x], other.at[x], other_sems.at[x]) for x in range(4)
     ]
-    for x in range(4):
-        copies[2 * x].start()
-        copies[2 * x + 1].start()
-        other_copies[x].start()
+
+    @pl.when(core == 0)
+    def _():
+        for copy in copies:
+            copy.start()
+
+    @pl.when(core != 0)
+    def _():
+        for copy in turned:
+            copy.start()
+
+    for copy in other_copies:
+        copy.start()
     queries = q_ref[...]
     of_row = lax.broadcasted_iota(jnp.int32, (ROWS, RES), 0) % REQ
     col = lax.broadcasted_iota(jnp.int32, (ROWS, RES), 1)
@@ -175,8 +225,8 @@
         copies[2 * x].wait()
         copies[2 * x + 1].wait()
         other_copies[x].wait()
-        total_part += dot_nn(po_ref[x], held[2 * x + core])
-        total_part += dot_nn(other[x], held[2 * x + 1 - core])
+        total_part += dot_nn(po_ref[x], held[2 * x + core].reshape(G * HD, 2 * HD))
+        total_part += dot_nn(other[x], held[2 * x + 1 - core].reshape(G * HD, 2 * HD))
     made = []
     for r in range(REQ):
         part = total_part[r * NB : (r + 1) * NB]
@@ -215,7 +265,7 @@
         in_specs=[scalar] * 4 + [vmem, hbm, hbm] + [vmem] * 4,
         out_specs=(vmem, vmem, vmem),
         scratch_shapes=[
-            pltpu.VMEM((8, G * HD, 2 * HD), BF),
+            pltpu.VMEM((8, 8, HD, 2 * HD), BF),
             pltpu.VMEM((4, REQ * NB, G * HD), BF),
             pltpu.SemaphoreType.DMA((8,)),
             pltpu.SemaphoreType.DMA((4,)),
@@ -279,6 +329,18 @@
     return pl.pallas_call(
         total_kernel, out_shape=jax.ShapeDtypeStruct((STEPS * REQ, HD), BF), name="total"
     )(pltpu.with_memory_space_constraint(parts, pltpu.VMEM))
+
+
+def lines(axes):
+    def device(z, y, x, c):
+        return ((z * 8 + y) * 4 + x) * 2 + c
+
+    return [
+        [device(i, j, x, c) if axes[c] == "z" else device(j, i, x, c) for i in range(8)]
+        for c in range(2)
+        for x in range(4)
+        for j in range(8)
+    ]
 
 
 def body(
@@ -301,11 +363,15 @@
     staged = stage(beacon_wk, beacon_wv)
     tails = tail(raw_k, raw_v)
     near = lax.ppermute(tails, SEQ, [(i, i + 1) for i in range(count - 1)])
-    column = lax.all_to_all(staged, "y", 0, 0).reshape(8 * HD, 2 * HD)
-    weights = lax.all_gather(column, "z", axis=0, tiled=True)
+    column = lax.all_to_all(staged, ALL, 0, 0, axis_index_groups=lines("yz"))
+    column = column.reshape(8 * HD, 2 * HD)
     at = jnp.stack([shard, lax.axis_index("c"), (shard == count - 1).astype(jnp.int32)])
     queries = jnp.transpose(beacon_queries[:, :, 0], (0, 2, 1, 3))
-    pooled = pool(at, phase, ratio, queries, raw_k, raw_v, near)
+    sums, stats = pool_own(at, phase, ratio, queries, raw_k, raw_v)
+    column, sums, stats = lax.optimization_barrier((column, sums, stats))
+    weights = lax.all_gather(column, ALL, axis=0, tiled=True, axis_index_groups=lines("zy"))
+    weights = weights.reshape(8, 8, HD, 2 * HD)
+    pooled = pool_rest(at, phase, ratio, queries, near, sums, stats)
     p_own = lax.all_to_all(pooled, "x", 0, 0)
     p_other = lax.ppermute(p_own, "c", [(0, 1), (1, 0)])
     step_queries = jnp.transpose(decode_queries[:, :, 0], (2, 0, 1, 3)).reshape(ROWS, HD)

time: 145 us -> 139 us (0.959)
  blocking collectives: 76.1 us -> 55.8 us
  starting transfers between devices: 16.9 us -> 24.9 us
  Pallas kernels: 15.4 us -> 21.5 us
  waiting for transfers between devices: 20.6 us -> 18.2 us
  local copies, waits for them, and re-layouts: 1.42 us -> 3.43 us
    all_to_all x1 -> x0, blocking collectives: 22.1 us -> none  [body(): column = lax.all_to_all(staged, 'y', 0, 0).reshape(8 * HD, 2 * HD)]
    all_to_all x0 -> x1, starting transfers between devices: none -> 10.9 us  [body(): column = lax.all_to_all(staged, ALL, 0, 0, axis_index_groups=lines('yz'))]
    all_gather x1, waiting for transfers between devices: 10.2 us -> 0.01 us  [body(): lax.all_gather(column, ALL, axis=0, tiled=True, axis_index_groups=lines('...]
    all_to_all x0 -> x1, waiting for transfers between devices: none -> 5.37 us  [body(): column = lax.all_to_all(staged, ALL, 0, 0, axis_index_groups=lines('yz'))]
    pallas_call x1 -> x2, Pallas kernels: 6.37 us -> 11.4 us  [the longest x1 6.53 us: pool_rest(): pl.pallas_call(rest_kernel, out_shape=jax.ShapeDtypeStruct((4, REQ * NB,...]
    ppermute x1, starting transfers between devices: 7.24 us -> 3.78 us  [body(): p_other = lax.ppermute(p_own, 'c', [(0, 1), (1, 0)])]
    all_to_all x1, blocking collectives: 12 us -> 15.3 us  [body(): parts = attend(lax.all_to_all(state, 'z', 0, 0), out_weight)]
    ppermute x1, waiting for transfers between devices: 3.08 us -> 5.48 us  [body(): near = lax.ppermute(tails, SEQ, [(i, i + 1) for i in range(count - 1)])]
  transfers between devices with their start and end apart: 4 -> 5, of which waited for: 4 -> 4; matrix products, arithmetic and copies ran while one was open for 1% -> 2% of each run, Pallas kernels for 5% -> 9%
where the time goes in v4:
time: 139 us; the launch traced here: 138 us
  blocking collectives  55.8 us (40%)
  starting transfers between devices  24.9 us (18%)
  Pallas kernels  21.5 us (15%)
  waiting for transfers between devices  18.2 us (13%)
  between operations  14.2 us (10%)
  local copies, waits for them, and re-layouts  3.43 us (2%)
    all_to_all x1, blocking collectives, body(): p_own = lax.all_to_all(pooled, 'x', 0, 0)  28.3 us
    all_to_all x1, blocking collectives, body(): parts = attend(lax.all_to_all(state, 'z', 0, 0), out_weight)  15.3 us
    all_to_all x1, blocking collectives, body(): state = combine(lax.all_to_all(state, 'y', 0, 0))  12.1 us
    all_to_all x1, starting transfers between devices, body(): column = lax.all_to_all(staged, ALL, 0, 0, axis_index_groups=lines('yz'))  10.9 us
    all_to_all x1, starting transfers between devices, body(): parts = lax.all_to_all(parts, ('x', 'c'), 0, 0)  7.28 us
    pallas_call x1, Pallas kernels, pool_rest(): pl.pallas_call(rest_kernel, out_shape=jax.ShapeDtypeStruct((4, REQ * NB,...  6.53 us
    ppermute x1, waiting for transfers between devices, body(): near = lax.ppermute(tails, SEQ, [(i, i + 1) for i in range(count - 1)])  5.48 us
    pallas_call x1, Pallas kernels, project_decode(): pl.pallas_call(decode_kernel, out_shape=(pltpu.VMEM((REQ, NB, HD), BF), p...  5.41 us
  transfers between devices with their start and end apart: 5, of which 4 were waited for; matrix products, arithmetic and copies ran while one was open for 2% of the time, Pallas kernels for 9%

profile of v4, /device:TPU:1, one launch (start us, length us, event | category | flops | bytes accessed | tf_op | source)
XLA Modules:
  0.0 138.1 jit_solution(187501322635741816)
XLA Ops:
  7.2 0.0 copy-start.1
  7.2 0.0 copy-start
  7.2 1.7 %stage.1 = bf16[8,128,256]{2,1,0:T(8,128)(2,1)} custom-call(bf16[128,128]{1,0:T(8,128)(2,1)} %wk_ref.1, bf16[128,128]{1,0:T(8,128)(2,1)} %wv_ref.1), custom_call_target="tpu_custom_call" | custom-call | tf_op jit(solution)/shard_map/stage/pallas_call | solution.py:42
  9.0 10.9 %all-to-all-start = ((bf16[8,128,256]{2,1,0:T(8,128)(2,1)}), bf16[8,128,256]{2,1,0:T(8,128)(2,1)}, u32[]{:S(2)}, u32[]{:S(2)}) async-start(bf16[8,128,256]{2,1,0:T(8,128)(2,1)} %stage.1), calls=%async_computation | async-start | bytes 1048576 | tf_op jit(solution)/shard_map/all_to_all | solution.py:366
  19.8 0.0 all-gather.2.cloned.1.call-start
  19.9 1.1 copy.20
  21.0 0.1 pad_add_fusion.at_ref
  21.1 4.9 %pool_own.1 = (f32[2,1024,128]{2,1,0:T(8,128)S(1)}, f32[2,1024,128]{2,1,0:T(8,128)S(1)}) custom-call(s32[3]{0:T(128)S(1)} %pad_add_fusion.at_ref, s32[2]{0:T(128)S(1)} %copy-done.8, s32[2,64]{1,0:T(2,128)S(1)} %copy-done.7, bf16[2,8,128,128]{3,2,1,0:T(8,128)(2,1)S(1)} %bitcast.27, bf16[2,1024,128]{2,1,0:T(8,128)(2,1)S(1)} %bitcast.30, ...), custom_call_target="tpu_custom_call" | custom-call | tf_op jit(solution)/shard_map/pool_own/pallas_call | solution.py:118
  26.0 1.0 copy-done.2
  27.0 5.4 %all-to-all-done = bf16[8,128,256]{2,1,0:T(8,128)(2,1)} async-done(((bf16[8,128,256]{2,1,0:T(8,128)(2,1)}), bf16[8,128,256]{2,1,0:T(8,128)(2,1)}, u32[]{:S(2)}, u32[]{:S(2)}) %all-to-all-start) | async-done | bytes 524320 | tf_op jit(solution)/shard_map/all_to_all | solution.py:366
  32.4 0.0 all-gather.2.cloned.1.call-update
  32.4 1.1 tail.1.tails_ref
  33.5 2.9 %collective-permute-start = (bf16[2,2,256,128]{3,2,1,0:T(8,128)(2,1)S(1)}, bf16[2,2,256,128]{3,2,1,0:T(8,128)(2,1)S(1)}, u32[]{:S(2)}, u32[]{:S(2)}) collective-permute-start(bf16[2,2,256,128]{3,2,1,0:T(8,128)(2,1)S(1)} %tail.1.tails_ref), channel_id=1, source_target_pairs={{0,8},{8,16},{16,24},{24,32},{32,40},{40,48},{48,56},{56,64},{64,7... | collective-permute-start | bytes 786440 | tf_op jit(solution)/shard_map/ppermute | solution.py:365
  36.4 5.5 %collective-permute-done.near_ref = bf16[2,2,256,128]{3,2,1,0:T(8,128)(2,1)S(1)} collective-permute-done((bf16[2,2,256,128]{3,2,1,0:T(8,128)(2,1)S(1)}, bf16[2,2,256,128]{3,2,1,0:T(8,128)(2,1)S(1)}, u32[]{:S(2)}, u32[]{:S(2)}) %collective-permute-start) | collective-permute-done | bytes 262176 | tf_op jit(solution)/shard_map/ppermute | solution.py:365
  41.9 6.5 %pool_rest.1 = bf16[4,256,1024]{2,1,0:T(8,128)(2,1)S(1)} custom-call(s32[3]{0:T(128)S(1)} %pad_add_fusion.at_ref, s32[2]{0:T(128)S(1)} %copy-done.8, s32[2,64]{1,0:T(2,128)S(1)} %copy-done.7, bf16[2,8,128,128]{3,2,1,0:T(8,128)(2,1)S(1)} %bitcast.28, bf16[2,2,256,128]{3,2,1,0:T(8,128)(2,1)S(1)} %collective-permute-done.near_ref, ...), custom_call_target="tpu_custom_call" | custom-call | tf_op jit(solution)/shard_map/pool_rest/pallas_call | solution.py:133
  48.4 0.0 copy-start.10
  48.4 0.0 copy-start.6
  48.5 0.0 copy-start.9
  48.5 28.3 %all_to_all.25.po_ref = bf16[4,256,1024]{2,1,0:T(8,128)(2,1)S(1)} all-to-all(bf16[4,256,1024]{2,1,0:T(8,128)(2,1)S(1)} %pool_rest.1), channel_id=1, replica_groups=mesh['z'=8,'y'=8,'x'=4,'c'=2] {'x'}, dimensions={0} | all-to-all | bytes 4194304 | tf_op jit(solution)/shard_map/all_to_all | solution.py:375
  76.8 3.8 %collective-permute-start.1 = (bf16[4,256,1024]{2,1,0:T(8,128)(2,1)S(1)}, bf16[4,256,1024]{2,1,0:T(8,128)(2,1)}, u32[]{:S(2)}, u32[]{:S(2)}) collective-permute-start(bf16[4,256,1024]{2,1,0:T(8,128)(2,1)S(1)} %all_to_all.25.po_ref), channel_id=1, source_target_pairs={{0,1},{1,0},{2,3},{3,2},{4,5},{5,4},{6,7},{7,6},{8,9},{9,8},{10,11... | collective-permute-start | bytes 6291464 | tf_op jit(solution)/shard_map/ppermute | solution.py:376
  80.6 3.9 %collective-permute-done.1.pt_ref = bf16[4,256,1024]{2,1,0:T(8,128)(2,1)} collective-permute-done((bf16[4,256,1024]{2,1,0:T(8,128)(2,1)S(1)}, bf16[4,256,1024]{2,1,0:T(8,128)(2,1)}, u32[]{:S(2)}, u32[]{:S(2)}) %collective-permute-start.1) | collective-permute-done | bytes 2097184 | tf_op jit(solution)/shard_map/ppermute | solution.py:376
  84.5 0.0 copy-start.4
  84.5 5.4 %project_decode.1 = (bf16[2,128,128]{2,1,0:T(8,128)(2,1)S(1)}, bf16[2,128,128]{2,1,0:T(8,128)(2,1)S(1)}, bf16[8,80,128]{2,1,0:T(8,128)(2,1)S(1)}) custom-call(s32[3]{0:T(128)S(1)} %pad_add_fusion.at_ref, s32[2]{0:T(128)S(1)} %copy-done.8, s32[2,64]{1,0:T(2,128)S(1)} %copy-done.7, s32[2,64]{1,0:T(2,128)S(1)} %copy-done.9, ...), custom_call_target="tpu_custom_call" | custom-call | tf_op jit(solution)/shard_map/project_decode/pallas_call | solution.py:258
  89.9 12.1 %all_to_all.26.in_ref = bf16[8,80,128]{2,1,0:T(8,128)(2,1)S(1)} all-to-all(bf16[8,80,128]{2,1,0:T(8,128)(2,1)S(1)} %get-tuple-element.18), channel_id=1, replica_groups=mesh['z'=8,'y'=8,'x'=4,'c'=2] {'y'}, dimensions={0} | all-to-all | bytes 327680 | tf_op jit(solution)/shard_map/all_to_all | solution.py:391
  102.0 0.3 combine.1
  102.3 15.3 %all_to_all.27.in_ref = bf16[8,80,128]{2,1,0:T(8,128)(2,1)S(1)} all-to-all(bf16[8,80,128]{2,1,0:T(8,128)(2,1)S(1)} %combine.1), channel_id=1, replica_groups=mesh['z'=8,'y'=8,'x'=4,'c'=2] {'z'}, dimensions={0} | all-to-all | bytes 327680 | tf_op jit(solution)/shard_map/all_to_all | solution.py:392
  117.7 1.0 attend.1
  118.7 7.3 %all-to-all-start.4 = ((bf16[8,16,128]{2,1,0:T(8,128)(2,1)}), bf16[8,16,128]{2,1,0:T(8,128)(2,1)S(1)}, u32[]{:S(2)}, u32[]{:S(2)}) async-start(bf16[8,16,128]{2,1,0:T(8,128)(2,1)} %attend.1), calls=%async_computation.4 | async-start | bytes 65536 | tf_op jit(solution)/shard_map/all_to_all | solution.py:393
  126.0 0.6 copy.21
  126.6 0.6 copy.22
  127.2 3.5 %all-to-all-done.4.in_ref = bf16[8,16,128]{2,1,0:T(8,128)(2,1)S(1)} async-done(((bf16[8,16,128]{2,1,0:T(8,128)(2,1)}), bf16[8,16,128]{2,1,0:T(8,128)(2,1)S(1)}, u32[]{:S(2)}, u32[]{:S(2)}) %all-to-all-start.4) | async-done | bytes 32800 | tf_op jit(solution)/shard_map/all_to_all | solution.py:393
  130.7 0.6 total.1
  (17 shorter events, 0.0 us)
Async XLA Ops:
  7.2 13.9 %copy-start.7 = (s32[2,64]{1,0:T(2,128)S(1)}, s32[2,64]{1,0:T(2,128)}, u32[]{:S(2)}) copy-start(s32[2,64]{1,0:T(2,128)} %ratio_ref.5) | copy-start | bytes 1540
  7.2 13.9 %copy-start.8 = (s32[2]{0:T(128)S(1)}, s32[2]{0:T(128)}, u32[]{:S(2)}) copy-start(s32[2]{0:T(128)} %phase_ref.5) | copy-start | bytes 28
  7.2 13.9 %copy-start.1 = (bf16[2,1024,1,128]{3,1,2,0:T(8,128)(2,1)S(1)}, bf16[2,1024,1,128]{3,1,2,0:T(8,128)(2,1)}, u32[]{:S(2)}) copy-start(bf16[2,1024,1,128]{3,1,2,0:T(8,128)(2,1)} %param.13) | copy-start | bytes 1572868
  7.2 13.9 %copy-start = (bf16[2,1024,1,128]{3,1,2,0:T(8,128)(2,1)S(1)}, bf16[2,1024,1,128]{3,1,2,0:T(8,128)(2,1)}, u32[]{:S(2)}) copy-start(bf16[2,1024,1,128]{3,1,2,0:T(8,128)(2,1)} %param.12) | copy-start | bytes 1572868
  9.0 23.4 %all-to-all-start = ((bf16[8,128,256]{2,1,0:T(8,128)(2,1)}), bf16[8,128,256]{2,1,0:T(8,128)(2,1)}, u32[]{:S(2)}, u32[]{:S(2)}) async-start(bf16[8,128,256]{2,1,0:T(8,128)(2,1)} %stage.1), calls=%async_computation | async-start | bytes 1048576 | tf_op jit(solution)/shard_map/all_to_all | solution.py:366
  19.8 64.6 %all-gather.2.cloned.1.call-start = ((), (), s32[]{:S(2)}) async-start(), calls=%async_computation.5 | async-start | bytes 4718592 | tf_op jit(solution)/shard_map/all_gather | solution.py:372
  26.0 1.0 copy-start.2
  32.4 9.5 %copy-start.3 = (f32[2,1024,128]{2,1,0:T(8,128)S(1)}, f32[2,1024,128]{2,1,0:T(8,128)}, u32[]{:S(2)}) copy-start(f32[2,1024,128]{2,1,0:T(8,128)} %copy-done.2) | copy-start | bytes 3145732
  33.5 8.4 %collective-permute-start = (bf16[2,2,256,128]{3,2,1,0:T(8,128)(2,1)S(1)}, bf16[2,2,256,128]{3,2,1,0:T(8,128)(2,1)S(1)}, u32[]{:S(2)}, u32[]{:S(2)}) collective-permute-start(bf16[2,2,256,128]{3,2,1,0:T(8,128)(2,1)S(1)} %tail.1.tails_ref), channel_id=1, source_target_pairs={{0,8},{8,16},{16,24},{24,32},{32,40},{40,48},{48,56},{56,64},{64,7... | collective-permute-start | bytes 786440 | tf_op jit(solution)/shard_map/ppermute | solution.py:365
  48.4 32.1 %copy-start.10 = (bf16[4,2,1,8,128]{4,3,2,1,0:T(8,128)(2,1)S(1)}, bf16[4,2,1,8,128]{4,3,2,1,0:T(8,128)(2,1)}, u32[]{:S(2)}) copy-start(bf16[4,2,1,8,128]{4,3,2,1,0:T(8,128)(2,1)} %param.22) | copy-start | bytes 49156
  48.4 36.0 %copy-start.5 = (bf16[2,256,1,128]{3,1,2,0:T(8,128)(2,1)S(1)}, bf16[2,256,1,128]{3,1,2,0:T(8,128)(2,1)}, u32[]{:S(2)}) copy-start(bf16[2,256,1,128]{3,1,2,0:T(8,128)(2,1)} %param.20) | copy-start | bytes 393220
  48.4 36.0 %copy-start.6 = (bf16[2,256,1,128]{3,1,2,0:T(8,128)(2,1)S(1)}, bf16[2,256,1,128]{3,1,2,0:T(8,128)(2,1)}, u32[]{:S(2)}) copy-start(bf16[2,256,1,128]{3,1,2,0:T(8,128)(2,1)} %param.21) | copy-start | bytes 393220
  48.5 36.0 %copy-start.9 = (s32[2,64]{1,0:T(2,128)S(1)}, s32[2,64]{1,0:T(2,128)}, u32[]{:S(2)}) copy-start(s32[2,64]{1,0:T(2,128)} %len_ref.1) | copy-start | bytes 1540
  76.8 7.7 %collective-permute-start.1 = (bf16[4,256,1024]{2,1,0:T(8,128)(2,1)S(1)}, bf16[4,256,1024]{2,1,0:T(8,128)(2,1)}, u32[]{:S(2)}, u32[]{:S(2)}) collective-permute-start(bf16[4,256,1024]{2,1,0:T(8,128)(2,1)S(1)} %all_to_all.25.po_ref), channel_id=1, source_target_pairs={{0,1},{1,0},{2,3},{3,2},{4,5},{5,4},{6,7},{7,6},{8,9},{9,8},{10,11... | collective-permute-start | bytes 6291464 | tf_op jit(solution)/shard_map/ppermute | solution.py:376
  84.5 33.2 %copy-start.4 = (bf16[1024,128]{1,0:T(8,128)(2,1)S(1)}, bf16[1024,128]{1,0:T(8,128)(2,1)}, u32[]{:S(2)}) copy-start(bf16[1024,128]{1,0:T(8,128)(2,1)} %w_ref.1) | copy-start | bytes 786436
  118.7 12.0 %all-to-all-start.4 = ((bf16[8,16,128]{2,1,0:T(8,128)(2,1)}), bf16[8,16,128]{2,1,0:T(8,128)(2,1)S(1)}, u32[]{:S(2)}, u32[]{:S(2)}) async-start(bf16[8,16,128]{2,1,0:T(8,128)(2,1)} %attend.1), calls=%async_computation.4 | async-start | bytes 65536 | tf_op jit(solution)/shard_map/all_to_all | solution.py:393
Sparse Core Ops, SparseCore 0:
  32.5 38.4 all-gather.1

commit v5 on v4

--- a/solution.py
+++ b/solution.py
@@ -79,29 +79,30 @@
 
 def own_kernel(at_ref, phase_ref, ratio_ref, q_ref, rk_ref, rv_ref, sum_ref, stat_ref):
     allowed = pool_bounds(at_ref, phase_ref, ratio_ref, OFF, INTERVAL)
-    lane = lax.broadcasted_iota(jnp.int32, (2 * NB, HD), 1)
     for pair in range(G // 2):
         q = q_ref[0, 2 * pair : 2 * pair + 2].reshape(2 * NB, HD)
         scores, peak = pool_rows(q, rk_ref[0], allowed)
         weights = jnp.exp2(scores - peak)
         total = jnp.sum(weights, axis=1, keepdims=True)
         rows = slice(2 * pair * NB, (2 * pair + 2) * NB)
-        sum_ref[0, rows] = dot_nn(weights.astype(BF), rv_ref[0])
-        stat_ref[0, rows] = jnp.where(lane == 0, peak, total)
+        sum_ref[0, rows] = (dot_nn(weights.astype(BF), rv_ref[0]) / total).astype(BF)
+        stat_ref[0, rows] = jnp.broadcast_to(peak + jnp.log2(total), (2 * NB, HD))
 
 
 def rest_kernel(at_ref, phase_ref, ratio_ref, q_ref, near_ref, sum_ref, stat_ref, out_ref):
     allowed = pool_bounds(at_ref, phase_ref, ratio_ref, 0, OFF)
+    values = jnp.concatenate([near_ref[1, 0], jnp.ones((OFF, HD), BF)], axis=1)
     for pair in range(G // 2):
         q = q_ref[0, 2 * pair : 2 * pair + 2].reshape(2 * NB, HD)
         scores, near_peak = pool_rows(q, near_ref[0, 0], allowed)
         rows = slice(2 * pair * NB, (2 * pair + 2) * NB)
-        own_peak, own_total = stat_ref[0, rows, 0:1], stat_ref[0, rows, 1:2]
-        peak = jnp.maximum(near_peak, own_peak)
-        weights = jnp.exp2(scores - peak)
-        factor = jnp.exp2(own_peak - peak)
-        total = jnp.sum(weights, axis=1, keepdims=True) + own_total * factor
-        weighted = dot_nn(weights.astype(BF), near_ref[1, 0]) + sum_ref[0, rows] * factor
+        own = stat_ref[0, rows]
+        peak = jnp.maximum(near_peak, own)
+        weights = jnp.exp2(scores - jnp.concatenate([peak, peak], axis=1)).astype(BF)
+        factor = jnp.exp2(own - peak)
+        both = dot_nn(weights, values)
+        total = both[:, HD:] + factor
+        weighted = both[:, :HD] + sum_ref[0, rows].astype(F32) * factor
         pooled = (weighted / total).astype(BF)
         for copy in range(4):
             for half in range(2):
@@ -117,7 +118,10 @@
     rows = pl.BlockSpec((1, INTERVAL, HD), lambda r, *_: (r, 0, 0))
     return pl.pallas_call(
         own_kernel,
-        out_shape=(jax.ShapeDtypeStruct((REQ, G * NB, HD), F32),) * 2,
+        out_shape=(
+            jax.ShapeDtypeStruct((REQ, G * NB, HD), BF),
+            jax.ShapeDtypeStruct((REQ, G * NB, HD), F32),
+        ),
         grid_spec=pltpu.PrefetchScalarGridSpec(
             num_scalar_prefetch=3,
             grid=(REQ,),
@@ -362,13 +366,13 @@
     raw_k, raw_v = raw_keys[:, :, 0], raw_values[:, :, 0]
     staged = stage(beacon_wk, beacon_wv)
     tails = tail(raw_k, raw_v)
-    near = lax.ppermute(tails, SEQ, [(i, i + 1) for i in range(count - 1)])
     column = lax.all_to_all(staged, ALL, 0, 0, axis_index_groups=lines("yz"))
     column = column.reshape(8 * HD, 2 * HD)
     at = jnp.stack([shard, lax.axis_index("c"), (shard == count - 1).astype(jnp.int32)])
     queries = jnp.transpose(beacon_queries[:, :, 0], (0, 2, 1, 3))
     sums, stats = pool_own(at, phase, ratio, queries, raw_k, raw_v)
-    column, sums, stats = lax.optimization_barrier((column, sums, stats))
+    column, sums, stats, tails = lax.optimization_barrier((column, sums, stats, tails))
+    near = lax.ppermute(tails, SEQ, [(i, i + 1) for i in range(count - 1)])
     weights = lax.all_gather(column, ALL, axis=0, tiled=True, axis_index_groups=lines("zy"))
     weights = weights.reshape(8, 8, HD, 2 * HD)
     pooled = pool_rest(at, phase, ratio, queries, near, sums, stats)

time: 139 us -> 133 us (0.957)
  Pallas kernels: 21.5 us -> 17.2 us
    pallas_call x1, Pallas kernels: 6.53 us -> 2.25 us  [pool_rest(): pl.pallas_call(rest_kernel, out_shape=jax.ShapeDtypeStruct((4, REQ * NB,...]
    unnamed x25 -> x21, local copies, waits for them, and re-layouts: 3.41 us -> 2.44 us
  transfers between devices with their start and end apart: 5 -> 5, of which waited for: 4 -> 4; matrix products, arithmetic and copies ran while one was open for 2% -> 2% of each run, Pallas kernels for 9% -> 6%
where the time goes in v5:
time: 133 us
  blocking collectives  55.8 us (42%)
  starting transfers between devices  24.8 us (19%)
  waiting for transfers between devices  18.1 us (14%)
  Pallas kernels  17.2 us (13%)
  between operations  14.2 us (11%)
  local copies, waits for them, and re-layouts  2.46 us (2%)
    all_to_all x1, blocking collectives, body(): p_own = lax.all_to_all(pooled, 'x', 0, 0)  28.3 us
    all_to_all x1, blocking collectives, body(): parts = attend(lax.all_to_all(state, 'z', 0, 0), out_weight)  15.4 us
    all_to_all x1, blocking collectives, body(): state = combine(lax.all_to_all(state, 'y', 0, 0))  12.1 us
    all_to_all x1, starting transfers between devices, body(): column = lax.all_to_all(staged, ALL, 0, 0, axis_index_groups=lines('yz'))  10.9 us
    all_to_all x1, starting transfers between devices, body(): parts = lax.all_to_all(parts, ('x', 'c'), 0, 0)  7.29 us
    ppermute x1, waiting for transfers between devices, body(): near = lax.ppermute(tails, SEQ, [(i, i + 1) for i in range(count - 1)])  5.48 us
    pallas_call x1, Pallas kernels, project_decode(): pl.pallas_call(decode_kernel, out_shape=(pltpu.VMEM((REQ, NB, HD), BF), p...  5.41 us
    all_to_all x1, waiting for transfers between devices, body(): column = lax.all_to_all(staged, ALL, 0, 0, axis_index_groups=lines('yz'))  5.27 us
  transfers between devices with their start and end apart: 5, of which 4 were waited for; matrix products, arithmetic and copies ran while one was open for 2% of the time, Pallas kernels for 6%

profile of v5, /device:TPU:1, one launch (start us, length us, event | category | flops | bytes accessed | tf_op | source)
XLA Modules:
  0.0 132.8 jit_solution(9409608590183990901)
XLA Ops:
  7.2 0.0 copy-start.1
  7.2 0.0 copy-start
  7.2 1.7 %stage.1 = bf16[8,128,256]{2,1,0:T(8,128)(2,1)} custom-call(bf16[128,128]{1,0:T(8,128)(2,1)} %wk_ref.1, bf16[128,128]{1,0:T(8,128)(2,1)} %wv_ref.1), custom_call_target="tpu_custom_call" | custom-call | tf_op jit(solution)/shard_map/stage/pallas_call | solution.py:42
  8.9 10.9 %all-to-all-start = ((bf16[8,128,256]{2,1,0:T(8,128)(2,1)}), bf16[8,128,256]{2,1,0:T(8,128)(2,1)}, u32[]{:S(2)}, u32[]{:S(2)}) async-start(bf16[8,128,256]{2,1,0:T(8,128)(2,1)} %stage.1), calls=%async_computation | async-start | bytes 1048576 | tf_op jit(solution)/shard_map/all_to_all | solution.py:369
  19.8 0.0 all-gather.2.cloned.1.call-start
  19.9 1.1 copy.20
  21.0 1.0 tail.1.tails_ref
  22.0 0.1 pad_add_fusion.at_ref
  22.1 5.0 %pool_own.1 = (bf16[2,1024,128]{2,1,0:T(8,128)(2,1)S(1)}, f32[2,1024,128]{2,1,0:T(8,128)S(1)}) custom-call(s32[3]{0:T(128)S(1)} %pad_add_fusion.at_ref, s32[2]{0:T(128)S(1)} %copy-done.6, s32[2,64]{1,0:T(2,128)S(1)} %copy-done.5, bf16[2,8,128,128]{3,2,1,0:T(8,128)(2,1)S(1)} %bitcast.27, bf16[2,1024,128]{2,1,0:T(8,128)(2,1)S(1)} %bitcast.30, ...), custom_call_target="tpu_custom_call" | custom-call | tf_op jit(solution)/shard_map/pool_own/pallas_call | solution.py:119
  27.1 5.3 %all-to-all-done = bf16[8,128,256]{2,1,0:T(8,128)(2,1)} async-done(((bf16[8,128,256]{2,1,0:T(8,128)(2,1)}), bf16[8,128,256]{2,1,0:T(8,128)(2,1)}, u32[]{:S(2)}, u32[]{:S(2)}) %all-to-all-start) | async-done | bytes 524320 | tf_op jit(solution)/shard_map/all_to_all | solution.py:369
  32.3 0.0 all-gather.2.cloned.1.call-update
  32.4 2.9 %collective-permute-start = (bf16[2,2,256,128]{3,2,1,0:T(8,128)(2,1)S(1)}, bf16[2,2,256,128]{3,2,1,0:T(8,128)(2,1)S(1)}, u32[]{:S(2)}, u32[]{:S(2)}) collective-permute-start(bf16[2,2,256,128]{3,2,1,0:T(8,128)(2,1)S(1)} %tail.1.tails_ref), channel_id=1, source_target_pairs={{0,8},{8,16},{16,24},{24,32},{32,40},{40,48},{48,56},{56,64},{64,7... | collective-permute-start | bytes 786440 | tf_op jit(solution)/shard_map/ppermute | solution.py:375
  35.3 5.5 %collective-permute-done.near_ref = bf16[2,2,256,128]{3,2,1,0:T(8,128)(2,1)S(1)} collective-permute-done((bf16[2,2,256,128]{3,2,1,0:T(8,128)(2,1)S(1)}, bf16[2,2,256,128]{3,2,1,0:T(8,128)(2,1)S(1)}, u32[]{:S(2)}, u32[]{:S(2)}) %collective-permute-start) | collective-permute-done | bytes 262176 | tf_op jit(solution)/shard_map/ppermute | solution.py:375
  40.8 2.3 %pool_rest.1 = bf16[4,256,1024]{2,1,0:T(8,128)(2,1)S(1)} custom-call(s32[3]{0:T(128)S(1)} %pad_add_fusion.at_ref, s32[2]{0:T(128)S(1)} %copy-done.6, s32[2,64]{1,0:T(2,128)S(1)} %copy-done.5, bf16[2,8,128,128]{3,2,1,0:T(8,128)(2,1)S(1)} %bitcast.28, bf16[2,2,256,128]{3,2,1,0:T(8,128)(2,1)S(1)} %collective-permute-done.near_ref, ...), custom_call_target="tpu_custom_call" | custom-call | tf_op jit(solution)/shard_map/pool_rest/pallas_call | solution.py:137
  43.0 0.0 copy-start.8
  43.1 0.0 copy-start.3
  43.1 0.0 copy-start.4
  43.1 0.0 copy-start.7
  43.1 28.3 %all_to_all.25.po_ref = bf16[4,256,1024]{2,1,0:T(8,128)(2,1)S(1)} all-to-all(bf16[4,256,1024]{2,1,0:T(8,128)(2,1)S(1)} %pool_rest.1), channel_id=1, replica_groups=mesh['z'=8,'y'=8,'x'=4,'c'=2] {'x'}, dimensions={0} | all-to-all | bytes 4194304 | tf_op jit(solution)/shard_map/all_to_all | solution.py:379
  71.4 3.7 %collective-permute-start.1 = (bf16[4,256,1024]{2,1,0:T(8,128)(2,1)S(1)}, bf16[4,256,1024]{2,1,0:T(8,128)(2,1)}, u32[]{:S(2)}, u32[]{:S(2)}) collective-permute-start(bf16[4,256,1024]{2,1,0:T(8,128)(2,1)S(1)} %all_to_all.25.po_ref), channel_id=1, source_target_pairs={{0,1},{1,0},{2,3},{3,2},{4,5},{5,4},{6,7},{7,6},{8,9},{9,8},{10,11... | collective-permute-start | bytes 6291464 | tf_op jit(solution)/shard_map/ppermute | solution.py:380
  75.2 3.9 %collective-permute-done.1.pt_ref = bf16[4,256,1024]{2,1,0:T(8,128)(2,1)} collective-permute-done((bf16[4,256,1024]{2,1,0:T(8,128)(2,1)S(1)}, bf16[4,256,1024]{2,1,0:T(8,128)(2,1)}, u32[]{:S(2)}, u32[]{:S(2)}) %collective-permute-start.1) | collective-permute-done | bytes 2097184 | tf_op jit(solution)/shard_map/ppermute | solution.py:380
  79.1 0.0 copy-start.2
  79.1 5.4 %project_decode.1 = (bf16[2,128,128]{2,1,0:T(8,128)(2,1)S(1)}, bf16[2,128,128]{2,1,0:T(8,128)(2,1)S(1)}, bf16[8,80,128]{2,1,0:T(8,128)(2,1)S(1)}) custom-call(s32[3]{0:T(128)S(1)} %pad_add_fusion.at_ref, s32[2]{0:T(128)S(1)} %copy-done.6, s32[2,64]{1,0:T(2,128)S(1)} %copy-done.5, s32[2,64]{1,0:T(2,128)S(1)} %copy-done.7, ...), custom_call_target="tpu_custom_call" | custom-call | tf_op jit(solution)/shard_map/project_decode/pallas_call | solution.py:262
  84.5 12.1 %all_to_all.26.in_ref = bf16[8,80,128]{2,1,0:T(8,128)(2,1)S(1)} all-to-all(bf16[8,80,128]{2,1,0:T(8,128)(2,1)S(1)} %get-tuple-element.20), channel_id=1, replica_groups=mesh['z'=8,'y'=8,'x'=4,'c'=2] {'y'}, dimensions={0} | all-to-all | bytes 327680 | tf_op jit(solution)/shard_map/all_to_all | solution.py:395
  96.7 0.3 combine.1
  96.9 15.4 %all_to_all.27.in_ref = bf16[8,80,128]{2,1,0:T(8,128)(2,1)S(1)} all-to-all(bf16[8,80,128]{2,1,0:T(8,128)(2,1)S(1)} %combine.1), channel_id=1, replica_groups=mesh['z'=8,'y'=8,'x'=4,'c'=2] {'z'}, dimensions={0} | all-to-all | bytes 327680 | tf_op jit(solution)/shard_map/all_to_all | solution.py:396
  112.3 1.0 attend.1
  113.3 7.3 %all-to-all-start.4 = ((bf16[8,16,128]{2,1,0:T(8,128)(2,1)}), bf16[8,16,128]{2,1,0:T(8,128)(2,1)S(1)}, u32[]{:S(2)}, u32[]{:S(2)}) async-start(bf16[8,16,128]{2,1,0:T(8,128)(2,1)} %attend.1), calls=%async_computation.4 | async-start | bytes 65536 | tf_op jit(solution)/shard_map/all_to_all | solution.py:397
  120.6 0.6 copy.21
  121.2 0.6 copy.22
  121.9 3.5 %all-to-all-done.4.in_ref = bf16[8,16,128]{2,1,0:T(8,128)(2,1)S(1)} async-done(((bf16[8,16,128]{2,1,0:T(8,128)(2,1)}), bf16[8,16,128]{2,1,0:T(8,128)(2,1)S(1)}, u32[]{:S(2)}, u32[]{:S(2)}) %all-to-all-start.4) | async-done | bytes 32800 | tf_op jit(solution)/shard_map/all_to_all | solution.py:397
  125.3 0.6 total.1
  (13 shorter events, 0.0 us)
Async XLA Ops:
  7.2 14.9 %copy-start.1 = (bf16[2,1024,1,128]{3,1,2,0:T(8,128)(2,1)S(1)}, bf16[2,1024,1,128]{3,1,2,0:T(8,128)(2,1)}, u32[]{:S(2)}) copy-start(bf16[2,1024,1,128]{3,1,2,0:T(8,128)(2,1)} %param.13) | copy-start | bytes 1572868
  7.2 14.9 %copy-start = (bf16[2,1024,1,128]{3,1,2,0:T(8,128)(2,1)S(1)}, bf16[2,1024,1,128]{3,1,2,0:T(8,128)(2,1)}, u32[]{:S(2)}) copy-start(bf16[2,1024,1,128]{3,1,2,0:T(8,128)(2,1)} %param.12) | copy-start | bytes 1572868
  7.2 14.9 %copy-start.5 = (s32[2,64]{1,0:T(2,128)S(1)}, s32[2,64]{1,0:T(2,128)}, u32[]{:S(2)}) copy-start(s32[2,64]{1,0:T(2,128)} %ratio_ref.5) | copy-start | bytes 1540
  7.2 14.9 %copy-start.6 = (s32[2]{0:T(128)S(1)}, s32[2]{0:T(128)}, u32[]{:S(2)}) copy-start(s32[2]{0:T(128)} %phase_ref.5) | copy-start | bytes 28
  8.9 23.4 %all-to-all-start = ((bf16[8,128,256]{2,1,0:T(8,128)(2,1)}), bf16[8,128,256]{2,1,0:T(8,128)(2,1)}, u32[]{:S(2)}, u32[]{:S(2)}) async-start(bf16[8,128,256]{2,1,0:T(8,128)(2,1)} %stage.1), calls=%async_computation | async-start | bytes 1048576 | tf_op jit(solution)/shard_map/all_to_all | solution.py:369
  19.8 59.3 %all-gather.2.cloned.1.call-start = ((), (), s32[]{:S(2)}) async-start(), calls=%async_computation.5 | async-start | bytes 4718592 | tf_op jit(solution)/shard_map/all_gather | solution.py:376
  32.4 8.4 %collective-permute-start = (bf16[2,2,256,128]{3,2,1,0:T(8,128)(2,1)S(1)}, bf16[2,2,256,128]{3,2,1,0:T(8,128)(2,1)S(1)}, u32[]{:S(2)}, u32[]{:S(2)}) collective-permute-start(bf16[2,2,256,128]{3,2,1,0:T(8,128)(2,1)S(1)} %tail.1.tails_ref), channel_id=1, source_target_pairs={{0,8},{8,16},{16,24},{24,32},{32,40},{40,48},{48,56},{56,64},{64,7... | collective-permute-start | bytes 786440 | tf_op jit(solution)/shard_map/ppermute | solution.py:375
  43.0 32.1 %copy-start.8 = (bf16[4,2,1,8,128]{4,3,2,1,0:T(8,128)(2,1)S(1)}, bf16[4,2,1,8,128]{4,3,2,1,0:T(8,128)(2,1)}, u32[]{:S(2)}) copy-start(bf16[4,2,1,8,128]{4,3,2,1,0:T(8,128)(2,1)} %param.22) | copy-start | bytes 49156
  43.1 36.0 %copy-start.3 = (bf16[2,256,1,128]{3,1,2,0:T(8,128)(2,1)S(1)}, bf16[2,256,1,128]{3,1,2,0:T(8,128)(2,1)}, u32[]{:S(2)}) copy-start(bf16[2,256,1,128]{3,1,2,0:T(8,128)(2,1)} %param.20) | copy-start | bytes 393220
  43.1 36.0 %copy-start.4 = (bf16[2,256,1,128]{3,1,2,0:T(8,128)(2,1)S(1)}, bf16[2,256,1,128]{3,1,2,0:T(8,128)(2,1)}, u32[]{:S(2)}) copy-start(bf16[2,256,1,128]{3,1,2,0:T(8,128)(2,1)} %param.21) | copy-start | bytes 393220
  43.1 36.0 %copy-start.7 = (s32[2,64]{1,0:T(2,128)S(1)}, s32[2,64]{1,0:T(2,128)}, u32[]{:S(2)}) copy-start(s32[2,64]{1,0:T(2,128)} %len_ref.1) | copy-start | bytes 1540
  71.4 7.6 %collective-permute-start.1 = (bf16[4,256,1024]{2,1,0:T(8,128)(2,1)S(1)}, bf16[4,256,1024]{2,1,0:T(8,128)(2,1)}, u32[]{:S(2)}, u32[]{:S(2)}) collective-permute-start(bf16[4,256,1024]{2,1,0:T(8,128)(2,1)S(1)} %all_to_all.25.po_ref), channel_id=1, source_target_pairs={{0,1},{1,0},{2,3},{3,2},{4,5},{5,4},{6,7},{7,6},{8,9},{9,8},{10,11... | collective-permute-start | bytes 6291464 | tf_op jit(solution)/shard_map/ppermute | solution.py:380
  79.1 33.2 %copy-start.2 = (bf16[1024,128]{1,0:T(8,128)(2,1)S(1)}, bf16[1024,128]{1,0:T(8,128)(2,1)}, u32[]{:S(2)}) copy-start(bf16[1024,128]{1,0:T(8,128)(2,1)} %w_ref.1) | copy-start | bytes 786436
  113.3 12.0 %all-to-all-start.4 = ((bf16[8,16,128]{2,1,0:T(8,128)(2,1)}), bf16[8,16,128]{2,1,0:T(8,128)(2,1)S(1)}, u32[]{:S(2)}, u32[]{:S(2)}) async-start(bf16[8,16,128]{2,1,0:T(8,128)(2,1)} %attend.1), calls=%async_computation.4 | async-start | bytes 65536 | tf_op jit(solution)/shard_map/all_to_all | solution.py:397
Sparse Core Ops, SparseCore 0:
  32.5 38.4 all-gather.1

commit v6 on v5

--- a/solution.py
+++ b/solution.py
@@ -392,8 +392,8 @@
         resident_values[:, :, 0],
         tails,
     )
-    state = combine(lax.all_to_all(state, "y", 0, 0))
-    parts = attend(lax.all_to_all(state, "z", 0, 0), out_weight)
+    state = combine(lax.all_to_all(state, ALL, 0, 0, axis_index_groups=lines("yz")))
+    parts = attend(lax.all_to_all(state, ALL, 0, 0, axis_index_groups=lines("zy")), out_weight)
     parts = lax.all_to_all(parts, ("x", "c"), 0, 0)
     projected = total(parts).reshape(STEPS, REQ, HD)
     return beacon_k[:, :, None], beacon_v[:, :, None], projected

time: 133 us -> 133 us (level)
  no operation moved by 1% of the time
where the time goes in v6:
time: 133 us
  blocking collectives  56 us (42%)
  starting transfers between devices  24.5 us (18%)
  waiting for transfers between devices  18.1 us (14%)
  Pallas kernels  17.2 us (13%)
  between operations  14.2 us (11%)
  local copies, waits for them, and re-layouts  2.46 us (2%)
    all_to_all x1, blocking collectives, body(): p_own = lax.all_to_all(pooled, 'x', 0, 0)  28.3 us
    all_to_all x1, blocking collectives, body(): lax.all_to_all(state, ALL, 0, 0, axis_index_groups=lines('yz'))  14.3 us
    all_to_all x1, blocking collectives, body(): lax.all_to_all(state, ALL, 0, 0, axis_index_groups=lines('zy'))  13.4 us
    all_to_all x1, starting transfers between devices, body(): column = lax.all_to_all(staged, ALL, 0, 0, axis_index_groups=lines('yz'))  10.9 us
    all_to_all x1, starting transfers between devices, body(): parts = lax.all_to_all(parts, ('x', 'c'), 0, 0)  6.93 us
    ppermute x1, waiting for transfers between devices, body(): near = lax.ppermute(tails, SEQ, [(i, i + 1) for i in range(count - 1)])  5.48 us
    pallas_call x1, Pallas kernels, project_decode(): pl.pallas_call(decode_kernel, out_shape=(pltpu.VMEM((REQ, NB, HD), BF), p...  5.41 us
    all_to_all x1, waiting for transfers between devices, body(): column = lax.all_to_all(staged, ALL, 0, 0, axis_index_groups=lines('yz'))  5.27 us
  transfers between devices with their start and end apart: 5, of which 4 were waited for; matrix products, arithmetic and copies ran while one was open for 2% of the time, Pallas kernels for 6%

profile of v6, /device:TPU:1, one launch (start us, length us, event | category | flops | bytes accessed | tf_op | source)
XLA Modules:
  0.0 132.6 jit_solution(16605907087855624817)
XLA Ops:
  7.2 0.0 copy-start.1
  7.2 0.0 copy-start
  7.2 1.7 %stage.1 = bf16[8,128,256]{2,1,0:T(8,128)(2,1)} custom-call(bf16[128,128]{1,0:T(8,128)(2,1)} %wk_ref.1, bf16[128,128]{1,0:T(8,128)(2,1)} %wv_ref.1), custom_call_target="tpu_custom_call" | custom-call | tf_op jit(solution)/shard_map/stage/pallas_call | solution.py:42
  8.9 10.9 %all-to-all-start = ((bf16[8,128,256]{2,1,0:T(8,128)(2,1)}), bf16[8,128,256]{2,1,0:T(8,128)(2,1)}, u32[]{:S(2)}, u32[]{:S(2)}) async-start(bf16[8,128,256]{2,1,0:T(8,128)(2,1)} %stage.1), calls=%async_computation | async-start | bytes 1048576 | tf_op jit(solution)/shard_map/all_to_all | solution.py:369
  19.8 0.0 all-gather.2.cloned.1.call-start
  19.9 1.1 copy.20
  21.0 1.0 tail.1.tails_ref
  22.0 0.1 pad_add_fusion.at_ref
  22.1 5.0 %pool_own.1 = (bf16[2,1024,128]{2,1,0:T(8,128)(2,1)S(1)}, f32[2,1024,128]{2,1,0:T(8,128)S(1)}) custom-call(s32[3]{0:T(128)S(1)} %pad_add_fusion.at_ref, s32[2]{0:T(128)S(1)} %copy-done.6, s32[2,64]{1,0:T(2,128)S(1)} %copy-done.5, bf16[2,8,128,128]{3,2,1,0:T(8,128)(2,1)S(1)} %bitcast.27, bf16[2,1024,128]{2,1,0:T(8,128)(2,1)S(1)} %bitcast.30, ...), custom_call_target="tpu_custom_call" | custom-call | tf_op jit(solution)/shard_map/pool_own/pallas_call | solution.py:119
  27.1 5.3 %all-to-all-done = bf16[8,128,256]{2,1,0:T(8,128)(2,1)} async-done(((bf16[8,128,256]{2,1,0:T(8,128)(2,1)}), bf16[8,128,256]{2,1,0:T(8,128)(2,1)}, u32[]{:S(2)}, u32[]{:S(2)}) %all-to-all-start) | async-done | bytes 524320 | tf_op jit(solution)/shard_map/all_to_all | solution.py:369
  32.3 0.0 all-gather.2.cloned.1.call-update
  32.4 2.9 %collective-permute-start = (bf16[2,2,256,128]{3,2,1,0:T(8,128)(2,1)S(1)}, bf16[2,2,256,128]{3,2,1,0:T(8,128)(2,1)S(1)}, u32[]{:S(2)}, u32[]{:S(2)}) collective-permute-start(bf16[2,2,256,128]{3,2,1,0:T(8,128)(2,1)S(1)} %tail.1.tails_ref), channel_id=1, source_target_pairs={{0,8},{8,16},{16,24},{24,32},{32,40},{40,48},{48,56},{56,64},{64,7... | collective-permute-start | bytes 786440 | tf_op jit(solution)/shard_map/ppermute | solution.py:375
  35.3 5.5 %collective-permute-done.near_ref = bf16[2,2,256,128]{3,2,1,0:T(8,128)(2,1)S(1)} collective-permute-done((bf16[2,2,256,128]{3,2,1,0:T(8,128)(2,1)S(1)}, bf16[2,2,256,128]{3,2,1,0:T(8,128)(2,1)S(1)}, u32[]{:S(2)}, u32[]{:S(2)}) %collective-permute-start) | collective-permute-done | bytes 262176 | tf_op jit(solution)/shard_map/ppermute | solution.py:375
  40.8 2.3 %pool_rest.1 = bf16[4,256,1024]{2,1,0:T(8,128)(2,1)S(1)} custom-call(s32[3]{0:T(128)S(1)} %pad_add_fusion.at_ref, s32[2]{0:T(128)S(1)} %copy-done.6, s32[2,64]{1,0:T(2,128)S(1)} %copy-done.5, bf16[2,8,128,128]{3,2,1,0:T(8,128)(2,1)S(1)} %bitcast.28, bf16[2,2,256,128]{3,2,1,0:T(8,128)(2,1)S(1)} %collective-permute-done.near_ref, ...), custom_call_target="tpu_custom_call" | custom-call | tf_op jit(solution)/shard_map/pool_rest/pallas_call | solution.py:137
  43.0 0.0 copy-start.8
  43.1 0.0 copy-start.3
  43.1 0.0 copy-start.4
  43.1 0.0 copy-start.7
  43.1 28.3 %all_to_all.25.po_ref = bf16[4,256,1024]{2,1,0:T(8,128)(2,1)S(1)} all-to-all(bf16[4,256,1024]{2,1,0:T(8,128)(2,1)S(1)} %pool_rest.1), channel_id=1, replica_groups=mesh['z'=8,'y'=8,'x'=4,'c'=2] {'x'}, dimensions={0} | all-to-all | bytes 4194304 | tf_op jit(solution)/shard_map/all_to_all | solution.py:379
  71.4 3.7 %collective-permute-start.1 = (bf16[4,256,1024]{2,1,0:T(8,128)(2,1)S(1)}, bf16[4,256,1024]{2,1,0:T(8,128)(2,1)}, u32[]{:S(2)}, u32[]{:S(2)}) collective-permute-start(bf16[4,256,1024]{2,1,0:T(8,128)(2,1)S(1)} %all_to_all.25.po_ref), channel_id=1, source_target_pairs={{0,1},{1,0},{2,3},{3,2},{4,5},{5,4},{6,7},{7,6},{8,9},{9,8},{10,11... | collective-permute-start | bytes 6291464 | tf_op jit(solution)/shard_map/ppermute | solution.py:380
  75.2 3.9 %collective-permute-done.1.pt_ref = bf16[4,256,1024]{2,1,0:T(8,128)(2,1)} collective-permute-done((bf16[4,256,1024]{2,1,0:T(8,128)(2,1)S(1)}, bf16[4,256,1024]{2,1,0:T(8,128)(2,1)}, u32[]{:S(2)}, u32[]{:S(2)}) %collective-permute-start.1) | collective-permute-done | bytes 2097184 | tf_op jit(solution)/shard_map/ppermute | solution.py:380
  79.1 0.0 copy-start.2
  79.1 5.4 %project_decode.1 = (bf16[2,128,128]{2,1,0:T(8,128)(2,1)S(1)}, bf16[2,128,128]{2,1,0:T(8,128)(2,1)S(1)}, bf16[8,80,128]{2,1,0:T(8,128)(2,1)S(1)}) custom-call(s32[3]{0:T(128)S(1)} %pad_add_fusion.at_ref, s32[2]{0:T(128)S(1)} %copy-done.6, s32[2,64]{1,0:T(2,128)S(1)} %copy-done.5, s32[2,64]{1,0:T(2,128)S(1)} %copy-done.7, ...), custom_call_target="tpu_custom_call" | custom-call | tf_op jit(solution)/shard_map/project_decode/pallas_call | solution.py:262
  84.5 14.3 %all_to_all.26.in_ref = bf16[8,80,128]{2,1,0:T(8,128)(2,1)S(1)} all-to-all(bf16[8,80,128]{2,1,0:T(8,128)(2,1)S(1)} %get-tuple-element.20), channel_id=1, replica_groups={{0,8,16,24,32,40,48,56},{64,72,80,88,96,104,112,120},{128,136,144,152,1..., dimensions={0} | all-to-all | bytes 327680 | tf_op jit(solution)/shard_map/all_to_all | solution.py:395
  98.8 0.3 combine.1
  99.0 13.4 %all_to_all.27.in_ref = bf16[8,80,128]{2,1,0:T(8,128)(2,1)S(1)} all-to-all(bf16[8,80,128]{2,1,0:T(8,128)(2,1)S(1)} %combine.1), channel_id=1, replica_groups={{0,64,128,192,256,320,384,448},{8,72,136,200,264,328,392,456},{16,80,14..., dimensions={0} | all-to-all | bytes 327680 | tf_op jit(solution)/shard_map/all_to_all | solution.py:396
  112.5 1.0 attend.1
  113.5 6.9 %all-to-all-start.4 = ((bf16[8,16,128]{2,1,0:T(8,128)(2,1)}), bf16[8,16,128]{2,1,0:T(8,128)(2,1)S(1)}, u32[]{:S(2)}, u32[]{:S(2)}) async-start(bf16[8,16,128]{2,1,0:T(8,128)(2,1)} %attend.1), calls=%async_computation.4 | async-start | bytes 65536 | tf_op jit(solution)/shard_map/all_to_all | solution.py:397
  120.4 0.6 copy.21
  121.0 0.6 copy.22
  121.7 3.5 %all-to-all-done.4.in_ref = bf16[8,16,128]{2,1,0:T(8,128)(2,1)S(1)} async-done(((bf16[8,16,128]{2,1,0:T(8,128)(2,1)}), bf16[8,16,128]{2,1,0:T(8,128)(2,1)S(1)}, u32[]{:S(2)}, u32[]{:S(2)}) %all-to-all-start.4) | async-done | bytes 32800 | tf_op jit(solution)/shard_map/all_to_all | solution.py:397
  125.2 0.6 total.1
  (13 shorter events, 0.0 us)
Async XLA Ops:
  7.2 14.9 %copy-start.1 = (bf16[2,1024,1,128]{3,1,2,0:T(8,128)(2,1)S(1)}, bf16[2,1024,1,128]{3,1,2,0:T(8,128)(2,1)}, u32[]{:S(2)}) copy-start(bf16[2,1024,1,128]{3,1,2,0:T(8,128)(2,1)} %param.13) | copy-start | bytes 1572868
  7.2 14.9 %copy-start = (bf16[2,1024,1,128]{3,1,2,0:T(8,128)(2,1)S(1)}, bf16[2,1024,1,128]{3,1,2,0:T(8,128)(2,1)}, u32[]{:S(2)}) copy-start(bf16[2,1024,1,128]{3,1,2,0:T(8,128)(2,1)} %param.12) | copy-start | bytes 1572868
  7.2 14.9 %copy-start.5 = (s32[2,64]{1,0:T(2,128)S(1)}, s32[2,64]{1,0:T(2,128)}, u32[]{:S(2)}) copy-start(s32[2,64]{1,0:T(2,128)} %ratio_ref.5) | copy-start | bytes 1540
  7.2 14.9 %copy-start.6 = (s32[2]{0:T(128)S(1)}, s32[2]{0:T(128)}, u32[]{:S(2)}) copy-start(s32[2]{0:T(128)} %phase_ref.5) | copy-start | bytes 28
  8.9 23.4 %all-to-all-start = ((bf16[8,128,256]{2,1,0:T(8,128)(2,1)}), bf16[8,128,256]{2,1,0:T(8,128)(2,1)}, u32[]{:S(2)}, u32[]{:S(2)}) async-start(bf16[8,128,256]{2,1,0:T(8,128)(2,1)} %stage.1), calls=%async_computation | async-start | bytes 1048576 | tf_op jit(solution)/shard_map/all_to_all | solution.py:369
  19.8 59.3 %all-gather.2.cloned.1.call-start = ((), (), s32[]{:S(2)}) async-start(), calls=%async_computation.5 | async-start | bytes 4718592 | tf_op jit(solution)/shard_map/all_gather | solution.py:376
  32.4 8.4 %collective-permute-start = (bf16[2,2,256,128]{3,2,1,0:T(8,128)(2,1)S(1)}, bf16[2,2,256,128]{3,2,1,0:T(8,128)(2,1)S(1)}, u32[]{:S(2)}, u32[]{:S(2)}) collective-permute-start(bf16[2,2,256,128]{3,2,1,0:T(8,128)(2,1)S(1)} %tail.1.tails_ref), channel_id=1, source_target_pairs={{0,8},{8,16},{16,24},{24,32},{32,40},{40,48},{48,56},{56,64},{64,7... | collective-permute-start | bytes 786440 | tf_op jit(solution)/shard_map/ppermute | solution.py:375
  43.0 32.1 %copy-start.8 = (bf16[4,2,1,8,128]{4,3,2,1,0:T(8,128)(2,1)S(1)}, bf16[4,2,1,8,128]{4,3,2,1,0:T(8,128)(2,1)}, u32[]{:S(2)}) copy-start(bf16[4,2,1,8,128]{4,3,2,1,0:T(8,128)(2,1)} %param.22) | copy-start | bytes 49156
  43.1 36.0 %copy-start.3 = (bf16[2,256,1,128]{3,1,2,0:T(8,128)(2,1)S(1)}, bf16[2,256,1,128]{3,1,2,0:T(8,128)(2,1)}, u32[]{:S(2)}) copy-start(bf16[2,256,1,128]{3,1,2,0:T(8,128)(2,1)} %param.20) | copy-start | bytes 393220
  43.1 36.0 %copy-start.4 = (bf16[2,256,1,128]{3,1,2,0:T(8,128)(2,1)S(1)}, bf16[2,256,1,128]{3,1,2,0:T(8,128)(2,1)}, u32[]{:S(2)}) copy-start(bf16[2,256,1,128]{3,1,2,0:T(8,128)(2,1)} %param.21) | copy-start | bytes 393220
  43.1 36.0 %copy-start.7 = (s32[2,64]{1,0:T(2,128)S(1)}, s32[2,64]{1,0:T(2,128)}, u32[]{:S(2)}) copy-start(s32[2,64]{1,0:T(2,128)} %len_ref.1) | copy-start | bytes 1540
  71.4 7.6 %collective-permute-start.1 = (bf16[4,256,1024]{2,1,0:T(8,128)(2,1)S(1)}, bf16[4,256,1024]{2,1,0:T(8,128)(2,1)}, u32[]{:S(2)}, u32[]{:S(2)}) collective-permute-start(bf16[4,256,1024]{2,1,0:T(8,128)(2,1)S(1)} %all_to_all.25.po_ref), channel_id=1, source_target_pairs={{0,1},{1,0},{2,3},{3,2},{4,5},{5,4},{6,7},{7,6},{8,9},{9,8},{10,11... | collective-permute-start | bytes 6291464 | tf_op jit(solution)/shard_map/ppermute | solution.py:380
  79.1 33.4 %copy-start.2 = (bf16[1024,128]{1,0:T(8,128)(2,1)S(1)}, bf16[1024,128]{1,0:T(8,128)(2,1)}, u32[]{:S(2)}) copy-start(bf16[1024,128]{1,0:T(8,128)(2,1)} %w_ref.1) | copy-start | bytes 786436
  113.5 11.7 %all-to-all-start.4 = ((bf16[8,16,128]{2,1,0:T(8,128)(2,1)}), bf16[8,16,128]{2,1,0:T(8,128)(2,1)S(1)}, u32[]{:S(2)}, u32[]{:S(2)}) async-start(bf16[8,16,128]{2,1,0:T(8,128)(2,1)} %attend.1), calls=%async_computation.4 | async-start | bytes 65536 | tf_op jit(solution)/shard_map/all_to_all | solution.py:397
Sparse Core Ops, SparseCore 0:
  32.5 38.4 all-gather.1
